TPU v7x, 32 devices: a whole 2x2x4 slice. The times are simulated.
32 devices in a mesh: dp: 8 (over z, y), tensor: 4 (over x, core).
Axes of the slice: x: 2, y: 2, z: 4, core: 2. Of those that a mesh axis runs over, the one named last changes fastest.
Arguments:
- tokens: bfloat16 [8192, 1536], P(('dp', 'tensor')), may hold values from -6 to 6
- gain_attn: float32 [1536], replicated, may hold values from 0.25 to 1.75
- query_weight: bfloat16 [1536, 1536], P(None, 'tensor'), may hold values from -0.21875 to 0.21875
- key_weight: bfloat16 [1536, 512], P(None, 'tensor'), may hold values from -0.15625 to 0.15625
- value_weight: bfloat16 [1536, 512], P(None, 'tensor'), may hold values from -0.15625 to 0.15625
- w_output: bfloat16 [1536, 1536], P('tensor'), may hold values from -0.875 to 0.875
- gain_ffn: float32 [1536], replicated, may hold values from 0.25 to 1.75
- w_router: bfloat16 [1536, 16], replicated, may hold values from -0.078125 to 0.078125
- w_gate: bfloat16 [16, 1536, 512], P('dp'), may hold values from -0.15625 to 0.15625
- w_up: bfloat16 [16, 1536, 512], P('dp'), may hold values from -0.15625 to 0.15625
- w_down: bfloat16 [16, 512, 1536], P('dp'), may hold values from -0.75 to 0.75
- segments: int32 [8, 1024], P('dp'), may hold values from 0 to 3, never falling along the last dimension, each value on 1 to 512 neighbouring positions
- routes: int32 [8192, 8], P(('dp', 'tensor')), may hold values from 0 to 15, all different within a row; in each aligned block of 256 rows (0 to 255, 256 to 511, ...) at most 160 rows name the same one
- cotangent: bfloat16 [8192, 1536], P(('dp', 'tensor')), may hold values from -6 to 6
Outputs:
- mixed: bfloat16 [8192, 1536], P(('dp', 'tensor'))
- grad_tokens: bfloat16 [8192, 1536], P(('dp', 'tensor'))
- grad_gain_attn: float32 [1536], replicated
- grad_query: float32 [1536, 1536], P(None, 'tensor')
- grad_key: float32 [1536, 512], P(None, 'tensor')
- grad_value: float32 [1536, 512], P(None, 'tensor')
- grad_output: float32 [1536, 1536], P('tensor')
- grad_gain_ffn: float32 [1536], replicated
- grad_router: float32 [1536, 16], replicated
- grad_gate: float32 [16, 1536, 512], P('dp')
- grad_up: float32 [16, 1536, 512], P('dp')
- grad_down: float32 [16, 512, 1536], P('dp')
Inputs may be any that keep to these rules, and one draw needn't show every extreme that they name: `routes`: each token names 8 different experts; of the tokens of one device no more than 160 name one expert, and in every draw some device's tokens name some expert exactly 160 times. `segments`: never falling along a sequence; each document covers 1 to 512 positions of its sequence, and some covers exactly 512.
All inputs are finite; a program needn't handle non-finite values.
Results may differ from a plain program's by a relative error of at most 0.024.
Values may be sent and summed in bfloat16 or wider, within the bound.
No kernel may reach another device: no remote copies, remote signals or barrier semaphores. Data moves between devices by JAX's collectives and lax.ppermute only.
A program may use at most 256 MiB of HBM per device.

v0:
```python
import math

import jax
import jax.numpy as jnp
from jax import lax
from jax.sharding import PartitionSpec as P

HEAD_WIDTH = 64


EPS = 1e-06
ROPE_BASE = 10000.0
NEG = -1e30
block_limit = 512


def rope_tables(length, head_size):
    half = head_size // 2
    freq = jnp.exp(-(jnp.arange(half, dtype=jnp.float32) * (2.0 / head_size)) * math.log(ROPE_BASE))
    angle = jnp.arange(length, dtype=jnp.float32)[:, None] * freq[None, :]
    return (jnp.cos(angle), jnp.sin(angle))


def rotate(value_rows, cos_tab, sin_tab):
    half = value_rows.shape[-1] // 2
    first = value_rows[..., :half]
    second = value_rows[..., half:]
    return jnp.concatenate(
        [first * cos_tab - second * sin_tab, second * cos_tab + first * sin_tab], axis=-1
    )


def row_norm(value_rows, gain_vec):
    inverse = lax.rsqrt(jnp.mean(value_rows * value_rows, axis=1, keepdims=True) + EPS)
    return (inverse, value_rows * inverse * gain_vec)


def norm_back(value_rows, inverse, gain_vec, upstream):
    scaled = upstream * gain_vec
    inner = jnp.mean(scaled * value_rows, axis=1, keepdims=True)
    return (
        inverse * scaled - value_rows * inverse**3 * inner,
        jnp.sum(upstream * value_rows * inverse, axis=0),
    )


def block_scores(query_block, key_seq, seg_block, seg_all, place_block, place_all, score_scale):
    scores = (
        jnp.einsum("qkgd,tkd->kgqt", query_block, key_seq, preferred_element_type=jnp.float32)
        * score_scale
    )
    allowed = (seg_block[:, None] == seg_all[None, :]) & (
        place_block[:, None] >= place_all[None, :]
    )
    return jnp.where(allowed, scores, NEG)


def on_device(
    tokens,
    gain_attn,
    query_weight,
    key_weight,
    value_weight,
    w_output,
    gain_ffn,
    w_router,
    w_gate,
    w_up,
    w_down,
    segments,
    routes,
    cotangent,
):
    rows_dev = tokens.shape[0]
    width = tokens.shape[1]
    data_count = lax.axis_size("dp")
    local_experts = w_gate.shape[0]
    expert_count = local_experts * data_count
    top_count = routes.shape[1]
    seq_count, seq_len = segments.shape
    kv_local = key_weight.shape[1] // HEAD_WIDTH
    query_group_width = query_weight.shape[1] // key_weight.shape[1]
    q_width = query_weight.shape[1]
    tok_rows = seq_count * seq_len
    capacity = 5 * rows_dev * top_count // (4 * expert_count)
    block_size = min(block_limit, seq_len)
    score_scale = HEAD_WIDTH ** (-0.5)
    cos_tab, sin_tab = rope_tables(seq_len, HEAD_WIDTH)
    cos_query = cos_tab[:, None, None, :]
    sin_query = sin_tab[:, None, None, :]
    cos_key = cos_tab[:, None, :]
    sin_key = sin_tab[:, None, :]
    places = jnp.arange(seq_len, dtype=jnp.int32)
    inputs = tokens.astype(jnp.float32)
    inverse_one, normed_float = row_norm(inputs, gain_attn)
    whole_one = lax.all_gather(normed_float.astype(jnp.bfloat16), "tensor", axis=0, tiled=True)
    query_projected = jnp.dot(whole_one, query_weight, preferred_element_type=jnp.float32).reshape(
        seq_count, seq_len, kv_local, query_group_width, HEAD_WIDTH
    )
    key_projected = jnp.dot(whole_one, key_weight, preferred_element_type=jnp.float32).reshape(
        seq_count, seq_len, kv_local, HEAD_WIDTH
    )
    value_rows = (
        jnp.dot(whole_one, value_weight, preferred_element_type=jnp.float32)
        .astype(jnp.bfloat16)
        .reshape(seq_count, seq_len, kv_local, HEAD_WIDTH)
    )
    queries = rotate(query_projected, cos_query, sin_query).astype(jnp.bfloat16)
    keys = rotate(key_projected, cos_key, sin_key).astype(jnp.bfloat16)

    def attend_forward(pieces):
        query_seq, key_seq, value_seq, seg_seq = pieces
        outputs = []
        totals = []
        for start_row in range(0, seq_len, block_size):
            stop_row = start_row + block_size
            scores = block_scores(
                query_seq[start_row:stop_row],
                key_seq,
                seg_seq[start_row:stop_row],
                seg_seq,
                places[start_row:stop_row],
                places,
                score_scale,
            )
            largest = jnp.max(scores, axis=-1, keepdims=True)
            shifted = jnp.exp(scores - largest)
            summed = jnp.sum(shifted, axis=-1, keepdims=True)
            probs = (shifted / summed).astype(jnp.bfloat16)
            outputs.append(
                jnp.einsum(
                    "kgqt,tkd->qkgd", probs, value_seq, preferred_element_type=jnp.float32
                ).astype(jnp.bfloat16)
            )
            totals.append((largest + jnp.log(summed))[..., 0])
        return (jnp.concatenate(outputs, axis=0), jnp.concatenate(totals, axis=2))

    attended, log_totals = lax.map(attend_forward, (queries, keys, value_rows, segments))
    attended_flat = attended.reshape(tok_rows, q_width)
    branch = lax.psum_scatter(
        jnp.dot(
            lax.slice_in_dim(attended_flat, 0, rows_dev * lax.axis_size("tensor"), axis=0),
            w_output,
            preferred_element_type=jnp.float32,
        ),
        "tensor",
        scatter_dimension=0,
        tiled=True,
    )
    residual = inputs + branch
    inverse_two, normed_two_float = row_norm(residual, gain_ffn)
    normed_two = normed_two_float.astype(jnp.bfloat16)
    logits = jnp.dot(normed_two, w_router, preferred_element_type=jnp.float32)
    expert_ids = jnp.arange(expert_count, dtype=jnp.int32)
    chosen = routes[:, :, None] == expert_ids[None, None, :]
    chosen_int = chosen.astype(jnp.int32)
    chosen_float = chosen.astype(jnp.float32)
    picked = jnp.sum(chosen_float * logits[:, None, :], axis=2)
    gates = jax.nn.softmax(picked, axis=1)
    per_row = jnp.sum(chosen_int, axis=1)
    earlier = jnp.cumsum(per_row, axis=0) - per_row
    slots = jnp.sum(chosen_int * earlier[:, None, :], axis=2)
    position = (routes * capacity + slots).reshape(-1)
    pair_count = rows_dev * top_count
    pair_of_slot = (
        jnp.full((expert_count * capacity,), pair_count, jnp.int32)
        .at[position]
        .set(jnp.arange(pair_count, dtype=jnp.int32))
    )
    row_of_slot = jnp.where(pair_of_slot < pair_count, pair_of_slot // top_count, rows_dev)
    zero_row = jnp.zeros((1, width), jnp.bfloat16)
    send_rows = jnp.concatenate([normed_two, zero_row], axis=0)[row_of_slot].reshape(
        data_count, local_experts, capacity, width
    )
    rows_in = lax.all_to_all(send_rows, "dp", split_axis=0, concat_axis=0, tiled=True)
    gate_pre = jnp.einsum("secd,edf->secf", rows_in, w_gate, preferred_element_type=jnp.float32)
    up_pre = jnp.einsum("secd,edf->secf", rows_in, w_up, preferred_element_type=jnp.float32)
    gate_pre, up_pre = (gate_pre, up_pre)
    hidden = (jax.nn.silu(gate_pre) * up_pre).astype(jnp.bfloat16)
    produced = jnp.einsum(
        "secf,efd->secd", hidden, w_down, preferred_element_type=jnp.float32
    ).astype(jnp.bfloat16)
    results = (produced, rows_in, gate_pre, up_pre)
    returned = lax.all_to_all(results[0], "dp", split_axis=0, concat_axis=0, tiled=True)
    expert_rows = returned.reshape(expert_count * capacity, width)[position].reshape(
        rows_dev, top_count, width
    )
    expert_float = expert_rows.astype(jnp.float32)
    mixed = (residual + jnp.sum(gates[:, :, None] * expert_float, axis=1)).astype(jnp.bfloat16)
    upstream = cotangent.astype(jnp.float32)
    d_expert = (
        (gates[:, :, None] * upstream[:, None, :]).astype(jnp.bfloat16).reshape(pair_count, width)
    )
    d_gates = jnp.sum(upstream[:, None, :] * expert_float, axis=2)
    d_send = jnp.concatenate([d_expert, zero_row], axis=0)[pair_of_slot].reshape(
        data_count, local_experts, capacity, width
    )
    rows_in = results[1]
    gate_pre = results[2]
    up_pre = results[3]
    d_received = lax.all_to_all(d_send, "dp", split_axis=0, concat_axis=0, tiled=True)
    sigmoid_gate = jax.nn.sigmoid(gate_pre)
    activated = gate_pre * sigmoid_gate
    hidden = (activated * up_pre).astype(jnp.bfloat16)
    d_hidden = jnp.einsum("secd,efd->secf", d_received, w_down, preferred_element_type=jnp.float32)
    grad_down = jnp.einsum("secf,secd->efd", hidden, d_received, preferred_element_type=jnp.float32)
    d_gate_pre = (
        d_hidden * up_pre * sigmoid_gate * (1.0 + gate_pre * (1.0 - sigmoid_gate))
    ).astype(jnp.bfloat16)
    d_up_pre = (d_hidden * activated).astype(jnp.bfloat16)
    grad_gate = jnp.einsum(
        "secd,secf->edf", rows_in, d_gate_pre, preferred_element_type=jnp.float32
    )
    grad_up = jnp.einsum("secd,secf->edf", rows_in, d_up_pre, preferred_element_type=jnp.float32)
    d_rows = (
        jnp.einsum("secf,edf->secd", d_gate_pre, w_gate, preferred_element_type=jnp.float32)
        + jnp.einsum("secf,edf->secd", d_up_pre, w_up, preferred_element_type=jnp.float32)
    ).astype(jnp.bfloat16)
    d_back = lax.all_to_all(d_rows, "dp", split_axis=0, concat_axis=0, tiled=True)
    d_copies = d_back.reshape(expert_count * capacity, width)[position].reshape(
        rows_dev, top_count, width
    )
    d_picked = gates * (d_gates - jnp.sum(gates * d_gates, axis=1, keepdims=True))
    d_logits = jnp.sum(chosen_float * d_picked[:, :, None], axis=1).astype(jnp.bfloat16)
    grad_router = jnp.einsum("rd,re->de", normed_two, d_logits, preferred_element_type=jnp.float32)
    d_normed_two = jnp.sum(d_copies.astype(jnp.float32), axis=1) + jnp.einsum(
        "re,de->rd", d_logits, w_router, preferred_element_type=jnp.float32
    )
    d_residual, gain_ffn_part = norm_back(residual, inverse_two, gain_ffn, d_normed_two)
    d_residual = d_residual + upstream
    whole_grad = lax.all_gather(d_residual.astype(jnp.bfloat16), "tensor", axis=0, tiled=True)
    d_attended = jnp.einsum(
        "td,fd->tf", whole_grad, w_output, preferred_element_type=jnp.float32
    ).astype(jnp.bfloat16)
    grad_output = jnp.einsum(
        "tf,td->fd", attended_flat, whole_grad, preferred_element_type=jnp.float32
    )
    d_attended_seq = d_attended.reshape(seq_count, seq_len, kv_local, query_group_width, HEAD_WIDTH)

    def attend_back(pieces):
        query_seq, key_seq, value_seq, seg_seq, total_seq, d_seq = pieces
        d_query_parts = []
        d_key_sum = jnp.zeros((seq_len, kv_local, HEAD_WIDTH), jnp.float32)
        d_value_sum = jnp.zeros((seq_len, kv_local, HEAD_WIDTH), jnp.float32)
        for start_row in range(0, seq_len, block_size):
            stop_row = start_row + block_size
            query_block = query_seq[start_row:stop_row]
            scores = block_scores(
                query_block,
                key_seq,
                seg_seq[start_row:stop_row],
                seg_seq,
                places[start_row:stop_row],
                places,
                score_scale,
            )
            probs = jnp.exp(scores - total_seq[:, :, start_row:stop_row, None])
            d_block = d_seq[start_row:stop_row]
            d_probs = jnp.einsum(
                "qkgd,tkd->kgqt", d_block, value_seq, preferred_element_type=jnp.float32
            )
            inner = jnp.sum(probs * d_probs, axis=-1, keepdims=True)
            d_scores = (probs * (d_probs - inner)).astype(jnp.bfloat16)
            d_query_parts.append(
                jnp.einsum("kgqt,tkd->qkgd", d_scores, key_seq, preferred_element_type=jnp.float32)
                * score_scale
            )
            d_key_sum = (
                d_key_sum
                + jnp.einsum(
                    "kgqt,qkgd->tkd", d_scores, query_block, preferred_element_type=jnp.float32
                )
                * score_scale
            )
            d_value_sum = d_value_sum + jnp.einsum(
                "kgqt,qkgd->tkd",
                probs.astype(jnp.bfloat16),
                d_block,
                preferred_element_type=jnp.float32,
            )
        return (jnp.concatenate(d_query_parts, axis=0), d_key_sum, d_value_sum)

    d_queries, d_keys, d_values = lax.map(
        attend_back, (queries, keys, value_rows, segments, log_totals, d_attended_seq)
    )
    d_query_lin = (
        rotate(d_queries, cos_query, -sin_query).astype(jnp.bfloat16).reshape(tok_rows, q_width)
    )
    d_key_lin = (
        rotate(d_keys, cos_key, -sin_key)
        .astype(jnp.bfloat16)
        .reshape(tok_rows, kv_local * HEAD_WIDTH)
    )
    d_value_lin = d_values.astype(jnp.bfloat16).reshape(tok_rows, kv_local * HEAD_WIDTH)
    grad_query = jnp.einsum("td,tf->df", whole_one, d_query_lin, preferred_element_type=jnp.float32)
    grad_key = jnp.einsum("td,tf->df", whole_one, d_key_lin, preferred_element_type=jnp.float32)
    grad_value = jnp.einsum("td,tf->df", whole_one, d_value_lin, preferred_element_type=jnp.float32)

    def take_rows(array):
        return lax.slice_in_dim(array, 0, lax.axis_size("tensor") * rows_dev, axis=0)

    total = jnp.einsum(
        "tf,df->td", take_rows(d_query_lin), query_weight, preferred_element_type=jnp.float32
    )
    total = total + jnp.einsum(
        "tf,df->td", take_rows(d_key_lin), key_weight, preferred_element_type=jnp.float32
    )
    d_normed_one = lax.psum_scatter(
        (
            total
            + jnp.einsum(
                "tf,df->td",
                take_rows(d_value_lin),
                value_weight,
                preferred_element_type=jnp.float32,
            )
        ).astype(jnp.bfloat16),
        "tensor",
        scatter_dimension=0,
        tiled=True,
    ).astype(jnp.float32)
    d_inputs, gain_attn_part = norm_back(inputs, inverse_one, gain_attn, d_normed_one)
    grad_tokens = (d_inputs + d_residual).astype(jnp.bfloat16)
    tensor_totals = (
        lax.psum(grad_gate.astype(jnp.bfloat16), "tensor").astype(jnp.float32),
        lax.psum(grad_up.astype(jnp.bfloat16), "tensor").astype(jnp.float32),
        lax.psum(grad_down.astype(jnp.bfloat16), "tensor").astype(jnp.float32),
        lax.psum(gain_attn_part.astype(jnp.bfloat16), "tensor").astype(jnp.float32),
        lax.psum(gain_ffn_part.astype(jnp.bfloat16), "tensor").astype(jnp.float32),
        lax.psum(grad_router.astype(jnp.bfloat16), "tensor").astype(jnp.float32),
    )
    data_totals = (
        lax.psum(grad_query.astype(jnp.bfloat16), "dp").astype(jnp.float32),
        lax.psum(grad_key.astype(jnp.bfloat16), "dp").astype(jnp.float32),
        lax.psum(grad_value.astype(jnp.bfloat16), "dp").astype(jnp.float32),
        lax.psum(grad_output.astype(jnp.bfloat16), "dp").astype(jnp.float32),
        lax.psum(tensor_totals[3].astype(jnp.bfloat16), "dp").astype(jnp.float32),
        lax.psum(tensor_totals[4].astype(jnp.bfloat16), "dp").astype(jnp.float32),
        lax.psum(tensor_totals[5].astype(jnp.bfloat16), "dp").astype(jnp.float32),
    )
    return (
        mixed,
        grad_tokens,
        data_totals[4],
        data_totals[0],
        data_totals[1],
        data_totals[2],
        data_totals[3],
        data_totals[5],
        data_totals[6],
        tensor_totals[0],
        tensor_totals[1],
        tensor_totals[2],
    )


def solution(mesh):
    in_specs = (
        P(("dp", "tensor"), None),
        P(),
        P(None, "tensor"),
        P(None, "tensor"),
        P(None, "tensor"),
        P("tensor", None),
        P(),
        P(),
        P("dp", None, None),
        P("dp", None, None),
        P("dp", None, None),
        P("dp", None),
        P(("dp", "tensor"), None),
        P(("dp", "tensor"), None),
    )
    out_specs = (
        P(("dp", "tensor"), None),
        P(("dp", "tensor"), None),
        P(),
        P(None, "tensor"),
        P(None, "tensor"),
        P(None, "tensor"),
        P("tensor", None),
        P(),
        P(),
        P("dp", None, None),
        P("dp", None, None),
        P("dp", None, None),
    )
    return jax.shard_map(
        on_device, mesh=mesh, in_specs=in_specs, out_specs=out_specs, check_vma=False
    )
```

profile of v0, /device:TPU:0, one launch (start us, length us, event | category | flops | bytes accessed | tf_op | source)
XLA Modules:
  0.0 1367.6 jit_solution(14065113369559017308)
XLA Ops:
  9.9 2.3 fusion.58
  14.2 2.5 fusion.50
  16.8 26.9 %all-gather.3.cloned.1.call-done = bf16[1024,1536]{1,0:T(8,128)(2,1)} async-done(((bf16[256,1536]{1,0:T(8,128)(2,1)}), bf16[1024,1536]{1,0:T(8,128)(2,1)}) %all-gather.3.cloned.1.call-update) | async-done | bytes 3145744 | tf_op jit(solution)/shard_map/all_gather | solution.py:96
  43.7 3.1 fusion.113
  46.9 3.7 fusion.114
  53.2 6.5 fusion.112
  65.3 2.4 fusion.83
  67.7 6.3 fusion.9
  74.0 6.0 fusion.82
  81.0 4.5 fusion.115
  86.8 8.1 scatter_custom_fusion
  94.9 49.1 %reduce-scatter.3.cloned.1.call-done = f32[256,1536]{1,0:T(8,128)} async-done(((f32[1024,1536]{1,0:T(8,128)}), f32[256,1536]{1,0:T(8,128)}) %reduce-scatter.3.cloned.1.call-update) | async-done | bytes 1572880 | tf_op jit(solution)/shard_map/reduce_scatter | solution.py:140
  149.1 18.0 %gather_fusion = bf16[2560,1536]{1,0:T(8,128)(2,1)} fusion(bf16[257,1536]{1,0:T(8,128)(2,1)} %concatenate.56, s32[3072]{0:T(1024)S(1)} %get-tuple-element.129), kind=kCustom, calls=%fused_computation | custom fusion | bytes 15738880 | tf_op jit(solution)/shard_map/gather | solution.py:172
  167.2 5.6 all-to-all-start
  172.8 2.5 convert_element_type.237
  177.1 3.2 fusion.8
  180.3 3.1 concatenate.57
  183.4 20.0 %gather_fusion.2 = bf16[2560,1536]{1,0:T(8,128)(2,1)} fusion(bf16[2049,1536]{1,0:T(8,128)(2,1)} %concatenate.57, s32[3072]{0:T(1024)S(1)} %get-tuple-element.128), kind=kCustom, calls=%fused_computation.2 | custom fusion | bytes 15738880 | tf_op jit(solution)/shard_map/gather | solution.py:195
  203.4 141.4 %all-to-all-done = bf16[8,2,160,1536]{3,2,1,0:T(8,128)(2,1)} async-done(((bf16[8,2,160,1536]{3,2,1,0:T(8,128)(2,1)}), bf16[8,2,160,1536]{3,2,1,0:T(8,128)(2,1)}, u32[]{:S(2)}, u32[]{:S(2)}) %all-to-all-start) | async-done | bytes 7864352 | tf_op jit(solution)/shard_map/all_to_all | solution.py:175
  344.8 4.9 all-to-all-start.2
  349.7 10.9 fusion.18
  360.6 9.2 fusion.20
  369.7 150.9 %all-to-all-done.2 = bf16[8,2,160,1536]{3,2,1,0:T(8,128)(2,1)} async-done(((bf16[8,2,160,1536]{3,2,1,0:T(8,128)(2,1)}), bf16[8,2,160,1536]{3,2,1,0:T(8,128)(2,1)}, u32[]{:S(2)}, u32[]{:S(2)}) %all-to-all-start.2) | async-done | bytes 7864352 | tf_op jit(solution)/shard_map/all_to_all | solution.py:201
  520.7 13.0 fusion.33
  535.2 6.4 convert_bitcast_fusion
  541.6 7.1 copy.105
  548.7 5.3 all-to-all-start.1
  554.0 9.6 fusion.43
  563.6 14.7 %fusion.13 = bf16[8,2,160,1536]{3,2,0,1:T(8,128)(2,1)} fusion(f32[2,8,160,1536]{3,2,1,0:T(8,128)} %fusion.43, bf16[8,2,160,512]{3,2,0,1:T(8,128)(2,1)} %get-tuple-element.92, bf16[2,1536,512]{2,1,0:T(8,128)(2,1)} %param.23), kind=kOutput, calls=%fused_computation.35 | convolution fusion | flops 4034396160 | bytes 29360128 | tf_op jit(solution)/shard_map/secf,edf->secd/dot_general | solution.py:217
  578.3 7.0 copy.108
  585.3 139.5 %all-to-all-done.1 = bf16[8,2,160,1536]{3,2,1,0:T(8,128)(2,1)} async-done(((bf16[8,2,160,1536]{3,2,1,0:T(8,128)(2,1)}), bf16[8,2,160,1536]{3,2,1,0:T(8,128)(2,1)}, u32[]{:S(2)}, u32[]{:S(2)}) %all-to-all-start.1) | async-done | bytes 7864352 | tf_op jit(solution)/shard_map/all_to_all | solution.py:184
  724.8 5.0 all-to-all-start.3
  729.9 17.8 %gather_fusion.1 = bf16[2048,1536]{1,0:T(8,128)(2,1)} fusion(bf16[2560,1536]{1,0:T(8,128)(2,1)} %bitcast.35, s32[2048]{0:T(1024)S(1)} %broadcast_clamp_fusion), kind=kCustom, calls=%fused_computation.1 | custom fusion | bytes 12591104 | tf_op jit(solution)/shard_map/gather | solution.py:185
  747.7 16.5 %fusion.1 = (f32[256,8]{1,0:T(8,128)S(1)}, f32[256,1536]{1,0:T(8,128)S(1)}) fusion(bf16[2048,1536]{1,0:T(8,128)(2,1)} %gather_fusion.1, f32[256,1536]{1,0:T(8,128)S(1)} %copy-done.7, f32[256,8]{1,0:T(8,128)S(1)} %copy.99), kind=kLoop, calls=%fused_computation.9 | loop fusion | flops 15333376 | bytes 9453568 | tf_op jit(solution)/shard_map/reduce_sum | solution.py:194
  764.4 136.4 %all-to-all-done.3 = bf16[8,2,160,1536]{3,2,1,0:T(8,128)(2,1)} async-done(((bf16[8,2,160,1536]{3,2,1,0:T(8,128)(2,1)}), bf16[8,2,160,1536]{3,2,1,0:T(8,128)(2,1)}, u32[]{:S(2)}, u32[]{:S(2)}) %all-to-all-start.3) | async-done | bytes 7864352 | tf_op jit(solution)/shard_map/all_to_all | solution.py:219
  900.7 17.9 %gather_fusion.3 = bf16[2048,1536]{1,0:T(8,128)(2,1)} fusion(bf16[2560,1536]{1,0:T(8,128)(2,1)} %bitcast.44, s32[2048]{0:T(1024)S(1)} %broadcast_clamp_fusion), kind=kCustom, calls=%fused_computation.3 | custom fusion | bytes 12591104 | tf_op jit(solution)/shard_map/gather | solution.py:220
  918.7 7.2 convert_reduce_fusion
  926.7 2.3 fusion.108
  929.1 10.1 bitcast_convert_fusion
  939.2 11.2 bitcast_convert_fusion.1
  950.4 10.8 bitcast_convert_fusion.2
  962.5 3.3 convolution_convert_fusion.5
  965.9 11.7 fusion.5
  978.6 10.8 fusion.7
  989.3 4.9 convolution_bitcast_fusion.1
  994.3 6.0 fusion.2
  1000.2 10.1 fusion.4
  1010.4 5.0 fusion.75
  1015.5 4.2 fusion.63
  1021.4 2.9 fusion.67
  1024.2 3.3 fusion.79
  1031.2 2.4 convolution_convert_fusion
  1033.6 2.9 convolution_convert_fusion.1
  1040.9 2.7 add_convert_fusion.1
  1043.6 86.5 %all-reduce.11.cloned.1.call-done = (bf16[2,1536,512]{2,1,0:T(8,128)(2,1)}, bf16[2,1536,512]{2,1,0:T(8,128)(2,1)}, bf16[2,512,1536]{2,1,0:T(8,128)(2,1)}) async-done(((bf16[2,1536,512]{2,1,0:T(8,128)(2,1)}, bf16[2,1536,512]{2,1,0:T(8,128)(2,1)}, bf16[2,512,1536]{2,1,0:T(8,128)(2,1)}), (bf16[2,1536,512]{2,1,0:T(8,128)(2,1)}, bf16[2,1536,512]{2,1,0:T(8,128)(2,1)}, ...) | async-done | bytes 9437200 | tf_op jit(solution)/shard_map/psum | solution.py:325
  1130.1 5.6 convert_element_type.274
  1135.8 3.6 convert_element_type.276
  1139.4 3.6 convert_element_type.278
  1143.2 122.3 %all-reduce.9.cloned.1.call-done = (bf16[1536,384]{1,0:T(8,128)(2,1)}, bf16[1536,128]{1,0:T(8,128)(2,1)}, bf16[1536,128]{1,0:T(8,128)(2,1)}, bf16[384,1536]{1,0:T(8,128)(2,1)}) async-done(((bf16[1536,384]{1,0:T(8,128)(2,1)}, bf16[1536,128]{1,0:T(8,128)(2,1)}, bf16[1536,128]{1,0:T(8,128)(2,1)}, bf16[384,1536]{1,0:T(8,128)(2,1)}), (bf16[1536,384]{1,0:T(8,128)(2,1)}, bf16[1536,128]{1,0:T(8,128)(2,1)}, ...) | async-done | bytes 3145744 | tf_op jit(solution)/shard_map/psum | solution.py:333
  1269.5 3.0 convert_element_type.262
  1274.1 30.7 %reduce-scatter.5.cloned.1.call-done = bf16[256,1536]{1,0:T(8,128)(2,1)} async-done(((bf16[1024,1536]{1,0:T(8,128)(2,1)}), bf16[256,1536]{1,0:T(8,128)(2,1)}) %reduce-scatter.5.cloned.1.call-update) | async-done | bytes 786448 | tf_op jit(solution)/shard_map/reduce_scatter | solution.py:308
  1306.6 10.7 all-reduce.4
  1317.4 37.8 %all-reduce.2 = (bf16[1536]{0:T(1024)(128)(2,1)S(1)}, bf16[1536]{0:T(1024)(128)(2,1)S(1)}, bf16[1536,16]{0,1:T(8,128)(2,1)S(1)}) all-reduce(bf16[1536]{0:T(1024)(128)(2,1)S(1)} %get-tuple-element.82, bf16[1536]{0:T(1024)(128)(2,1)S(1)} %get-tuple-element.83, ...), channel_id=1, replica_groups=mesh['dp'=8,'tensor'=4] {'dp'}, use_global_device_ids=true, to_apply=%region_27.28 | all-reduce | flops 27648 | bytes 110592 | tf_op jit(solution)/shard_map/psum | solution.py:337
  1357.1 3.2 fusion.55
  (230 shorter events, 46.1 us)
Async XLA Ops:
  7.2 513.5 %copy-start = (bf16[2,512,1536]{2,1,0:T(8,128)(2,1)S(1)}, bf16[2,512,1536]{2,1,0:T(8,128)(2,1)}, u32[]{:S(2)}) copy-start(bf16[2,512,1536]{2,1,0:T(8,128)(2,1)} %param.24) | copy-start | bytes 9437188
  7.2 36.5 %all-gather.3.cloned.1.call-start = ((), (), s32[]{:S(2)}) async-start(), calls=%async_computation.6 | async-start | bytes 3932160 | tf_op jit(solution)/shard_map/all_gather | solution.py:96
  12.2 131.8 %reduce-scatter.3.cloned.1.call-start = ((), (), s32[]{:S(2)}) async-start(), calls=%async_computation.7 | async-start | bytes 7864320 | tf_op jit(solution)/shard_map/reduce_scatter | solution.py:140
  14.2 36.4 %copy-start.16 = (f32[1024,32]{0,1:T(8,128)}, f32[1024,32]{0,1:T(8,128)S(1)}, u32[]{:S(2)}) copy-start(f32[1024,32]{0,1:T(8,128)S(1)} %get-tuple-element.118) | copy-start | bytes 393220
  46.8 6.3 copy-start.28
  46.9 6.3 copy-start.30
  46.9 4.0 copy-start.38
  53.1 12.2 copy-start.2
  53.2 12.2 copy-start.44
  59.7 14.2 %copy-start.46 = (f32[2,3,512]{2,1,0:T(4,128)}, f32[2,3,512]{2,1,0:T(4,128)S(1)}, u32[]{:S(2)}) copy-start(f32[2,3,512]{2,1,0:T(4,128)S(1)} %get-tuple-element.121) | copy-start | bytes 36868
  59.7 3.4 copy-start.3
  63.1 4.6 copy-start.48
  65.3 8.7 copy-start.23
  74.0 6.0 copy-start.50
  74.0 7.0 copy-start.34
  81.0 4.6 copy-start.39
  85.5 61.6 %copy-start.42 = (f32[1536]{0:T(1024)S(1)}, f32[1536]{0:T(1024)}, u32[]{:S(2)}) copy-start(f32[1536]{0:T(1024)} %param.20) | copy-start | bytes 18436
  146.6 20.6 %copy-start.52 = (f32[256]{0:T(256)}, f32[256]{0:T(256)S(1)}, u32[]{:S(2)}) copy-start(f32[256]{0:T(256)S(1)} %get-tuple-element.115) | copy-start | bytes 3076
  167.2 8.1 copy-start.40
  167.2 177.6 %all-to-all-start = ((bf16[8,2,160,1536]{3,2,1,0:T(8,128)(2,1)}), bf16[8,2,160,1536]{3,2,1,0:T(8,128)(2,1)}, u32[]{:S(2)}, u32[]{:S(2)}) async-start(bf16[8,2,160,1536]{3,2,1,0:T(8,128)(2,1)} %bitcast.264), calls=%async_computation.1 | async-start | bytes 15728640 | tf_op jit(solution)/shard_map/all_to_all | solution.py:175
  344.8 175.9 %all-to-all-start.2 = ((bf16[8,2,160,1536]{3,2,1,0:T(8,128)(2,1)}), bf16[8,2,160,1536]{3,2,1,0:T(8,128)(2,1)}, u32[]{:S(2)}, u32[]{:S(2)}) async-start(bf16[8,2,160,1536]{3,2,1,0:T(8,128)(2,1)} %bitcast.265), calls=%async_computation.3 | async-start | bytes 15728640 | tf_op jit(solution)/shard_map/all_to_all | solution.py:201
  349.7 10.9 copy-start.58
  548.7 5.3 copy-start.59
  548.7 176.1 %all-to-all-start.1 = ((bf16[8,2,160,1536]{3,2,1,0:T(8,128)(2,1)}), bf16[8,2,160,1536]{3,2,1,0:T(8,128)(2,1)}, u32[]{:S(2)}, u32[]{:S(2)}) async-start(bf16[8,2,160,1536]{3,2,1,0:T(8,128)(2,1)} %copy.105), calls=%async_computation.2 | async-start | bytes 15728640 | tf_op jit(solution)/shard_map/all_to_all | solution.py:184
  724.8 175.9 %all-to-all-start.3 = ((bf16[8,2,160,1536]{3,2,1,0:T(8,128)(2,1)}), bf16[8,2,160,1536]{3,2,1,0:T(8,128)(2,1)}, u32[]{:S(2)}, u32[]{:S(2)}) async-start(bf16[8,2,160,1536]{3,2,1,0:T(8,128)(2,1)} %copy.108), calls=%async_computation.4 | async-start | bytes 15728640 | tf_op jit(solution)/shard_map/all_to_all | solution.py:219
  729.8 231.5 %all-gather.5.cloned.1.call-start = ((), (), s32[]{:S(2)}) async-start(), calls=%async_computation.8 | async-start | bytes 3932160 | tf_op jit(solution)/shard_map/all_gather | solution.py:231
  729.8 17.8 %copy-start.7 = (f32[256,1536]{1,0:T(8,128)S(1)}, f32[256,1536]{1,0:T(8,128)}, u32[]{:S(2)}) copy-start(f32[256,1536]{1,0:T(8,128)} %convert_element_type.237) | copy-start | bytes 4718596
  918.6 7.2 copy-start.6
  918.6 7.2 copy-start.43
  918.6 7.2 copy-start.53
  918.6 8.0 copy-start.18
  918.7 8.0 copy-start.56
  928.9 201.2 %all-reduce.11.cloned.1.call-start = ((), (), s32[]{:S(2)}) async-start(), calls=%async_computation.11 | async-start | bytes 18874368 | tf_op jit(solution)/shard_map/psum | solution.py:325
  929.1 10.1 copy-start.61
  939.2 11.2 copy-start.62
  961.2 4.6 copy-start.24
  961.2 304.3 %all-reduce.9.cloned.1.call-start = ((), (), s32[]{:S(2)}) async-start(), calls=%async_computation.10 | async-start | bytes 6291456 | tf_op jit(solution)/shard_map/psum | solution.py:333
  965.8 11.7 slice-start.3
  965.8 11.7 slice-start.4
  965.8 12.7 slice-start.5
  977.5 16.7 %slice-start = ((s8[12582912]{0:T(1024)(128)(4,1)}), s8[4194304]{0:T(1024)(128)(4,1)S(1)}, s32[]{:S(2)}) async-start(s8[12582912]{0:T(1024)(128)(4,1)} %bitcast.258), calls=%async_computation.12 | async-start | bytes 8388608
  978.6 10.8 copy-start.13
  978.6 10.8 copy-start.15
  978.6 15.7 %slice-start.1 = ((s8[12582912]{0:T(1024)(128)(4,1)}), s8[4194304]{0:T(1024)(128)(4,1)S(1)}, s32[]{:S(2)}) async-start(s8[12582912]{0:T(1024)(128)(4,1)} %bitcast.258), calls=%async_computation.13 | async-start | bytes 8388608
  978.6 15.7 %slice-start.2 = ((s8[12582912]{0:T(1024)(128)(4,1)}), s8[4194304]{0:T(1024)(128)(4,1)S(1)}, s32[]{:S(2)}) async-start(s8[12582912]{0:T(1024)(128)(4,1)} %bitcast.258), calls=%async_computation.14 | async-start | bytes 8388608
  1010.3 5.0 copy-start.17
  1010.3 5.0 copy-start.36
  1010.3 5.1 copy-start.29
  1010.3 5.1 copy-start.31
  1010.3 9.3 slice-start.6
  1015.3 4.4 slice-start.7
  1021.4 12.2 copy-start.10
  1027.5 6.1 copy-start.25
  1027.5 3.6 copy-start.22
  1027.5 3.6 copy-start.60
  1036.5 268.3 %reduce-scatter.5.cloned.1.call-start = ((), (), s32[]{:S(2)}) async-start(), calls=%async_computation.9 | async-start | bytes 3932160 | tf_op jit(solution)/shard_map/reduce_scatter | solution.py:308
  1130.1 5.6 copy-start.20
  1135.8 3.6 copy-start.19
  1139.4 3.6 copy-start.9
  1143.0 161.8 %copy-start.41 = (f32[1536]{0:T(1024)S(1)}, f32[1536]{0:T(1024)}, u32[]{:S(2)}) copy-start(f32[1536]{0:T(1024)} %param.15) | copy-start | bytes 18436
  1143.0 161.8 %copy-start.55 = (f32[256]{0:T(256)S(1)}, f32[256]{0:T(256)}, u32[]{:S(2)}) copy-start(f32[256]{0:T(256)} %copy-done.54) | copy-start | bytes 3076
  1265.5 6.9 copy-start.33
  1267.5 89.5 %copy-start.57 = (f32[256]{0:T(256)S(1)}, f32[256]{0:T(256)}, u32[]{:S(2)}) copy-start(f32[256]{0:T(256)} %get-tuple-element.112) | copy-start | bytes 3076
  1269.5 90.8 %copy-start.1 = (bf16[2,512,1536]{2,1,0:T(8,128)(2,1)S(1)}, bf16[2,512,1536]{2,1,0:T(8,128)(2,1)}, u32[]{:S(2)}) copy-start(bf16[2,512,1536]{2,1,0:T(8,128)(2,1)} %param.24) | copy-start | bytes 9437188
  (18 other events, 34.9 us)
Sparse Core Ops, SparseCore 0:
  12.4 31.2 all-gather.2
  85.7 58.3 reduce-scatter.2
  929.1 26.7 all-gather.4
  961.3 168.7 all-reduce.10
  1134.9 130.5 all-reduce.8
  1267.9 36.8 reduce-scatter.4
where the time goes:
time: 1370 us
  waiting for transfers between devices  884 us (65%)
  matrix products  187 us (14%)
  local copies, waits for them, and re-layouts  110 us (8%)
  other arithmetic  102 us (7%)
  blocking collectives  48.6 us (4%)
  starting transfers between devices  21.3 us (2%)
  between operations  15.7 us (1%)
    all_to_all x1, waiting for transfers between devices, on_device(): lax.all_to_all(d_send, 'dp', split_axis=0, concat_axis=0, tiled=True)  151 us
    all_to_all x1, waiting for transfers between devices, on_device(): lax.all_to_all(send_rows, 'dp', split_axis=0, concat_axis=0, tiled=True)  141 us
    all_to_all x1, waiting for transfers between devices, on_device(): lax.all_to_all(results[0], 'dp', split_axis=0, concat_axis=0, tiled=True)  139 us
    all_to_all x1, waiting for transfers between devices, on_device(): lax.all_to_all(d_rows, 'dp', split_axis=0, concat_axis=0, tiled=True)  136 us
    psum x1, waiting for transfers between devices, on_device(): lax.psum(grad_query.astype(jnp.bfloat16), 'dp').astype(jnp.float32)  122 us
    psum x1, waiting for transfers between devices, on_device(): lax.psum(grad_gate.astype(jnp.bfloat16), 'tensor').astype(jnp.float32)  86.5 us
    reduce_scatter x1, waiting for transfers between devices, on_device(): lax.psum_scatter(jnp.dot(lax.slice_in_dim(attended_flat, 0, rows_dev * la...  49.1 us
    psum x1, blocking collectives, on_device(): lax.psum(tensor_totals[3].astype(jnp.bfloat16), 'dp').astype(jnp.float32)  37.8 us
  transfers between devices with their start and end apart: 10, of which 9 were waited for; matrix products, arithmetic and copies ran while one was open for 19% of the time, Pallas kernels for 0%

commit v1 on v0

v1 whole, which is shorter than its diff:
```python
import functools
import math

import jax
import jax.numpy as jnp
import numpy as np
from jax import lax
from jax.experimental import pallas as pl
from jax.experimental.pallas import tpu as pltpu
from jax.sharding import PartitionSpec as P

HEAD_WIDTH = 64
EPS = 1e-06
ROPE_BASE = 10000.0
NEG = -1e30
LANES = 128
BLOCK = 256
REACH = 512
VMEM_BYTES = 52 * 1024 * 1024
low = jnp.bfloat16
wide = jnp.float32
NN = (((1,), (0,)), ((), ()))
NT = (((1,), (1,)), ((), ()))
TN = (((0,), (0,)), ((), ()))
dot = functools.partial(lax.dot_general, preferred_element_type=jnp.float32)
Shape = jax.ShapeDtypeStruct
ANY = pl.BlockSpec(memory_space=pl.ANY)
VMEM = pl.BlockSpec(memory_space=pltpu.VMEM)
SMEM = pl.BlockSpec(memory_space=pltpu.SMEM)


def rope_tables(length):
    half = HEAD_WIDTH // 2
    freq = np.exp(-(np.arange(half, dtype=np.float32) * (2.0 / HEAD_WIDTH)) * math.log(ROPE_BASE))
    angle = np.arange(length, dtype=np.float32)[:, None] * freq.astype(np.float32)[None, :]
    cos, sin = np.cos(angle), np.sin(angle)
    cos = np.concatenate([cos] * 4, axis=1).astype(np.float32)
    sin = np.concatenate([-sin, sin, -sin, sin], axis=1).astype(np.float32)
    return jnp.asarray(cos), jnp.asarray(sin)


def ring_order(count):
    return list(range(0, count, 2)) + list(range(count - 1, 0, -2))


def ring_send(array, step):
    count = lax.axis_size("dp")
    order = ring_order(count)
    return lax.ppermute(
        array, "dp", [(order[i], order[(i + step) % count]) for i in range(count)]
    )


def ring_places():
    count = lax.axis_size("dp")
    order = ring_order(count)
    place = jnp.asarray([order.index(i) for i in range(count)], jnp.int32)
    return (place[lax.axis_index("dp")] + jnp.arange(count, dtype=jnp.int32)) % count


def ring_gather(array, opposite=None):
    count = lax.axis_size("dp")
    half = array.shape[0] // 2
    below, above = [], []
    up, down = array, array
    for _ in range(count // 2 - 1):
        up = ring_send(up, 1)
        down = ring_send(down, -1)
        below.append(up)
        above.append(down)
    top = ring_send(up[:half], 1)
    bottom = ring_send(down[half:], -1)
    return below, above, (top, bottom)


def add_low(first, second):
    return (first.astype(wide) + second.astype(wide)).astype(low)


def ring_scatter(below, above, opposite):
    up_half, down_half = opposite
    half = up_half.shape[0]
    up = ring_send(up_half, 1)
    down = ring_send(down_half, -1)
    for k in range(len(above), 0, -1):
        part_up, part_down = above[k - 1], below[k - 1]
        if k == len(above):
            up = jnp.concatenate([add_low(up, part_up[:half]), part_up[half:]], axis=0)
            down = jnp.concatenate([part_down[:half], add_low(down, part_down[half:])], axis=0)
        else:
            up = add_low(up, part_up)
            down = add_low(down, part_down)
        up = ring_send(up, 1)
        down = ring_send(down, -1)
    return up, down


def swap(array, axis, mask):
    return lax.ppermute(array, axis, [(i, i ^ mask) for i in range(lax.axis_size(axis))])


def cube_sum(array, axes):
    for axis in axes:
        mask = 1
        while mask < lax.axis_size(axis):
            array = array + swap(array, axis, mask)
            mask *= 2
    return array


def tensor_blocks(array):
    far = swap(array, "tensor", 2)
    return array, swap(array, "tensor", 1), far, swap(far, "tensor", 1)


def call(body, operands, in_specs, out_specs, out_shape, scratch=(), grid=None, after=(), name=None, cost=None, alias=None):
    count = len(after)
    position = len(operands)

    def kernel(*refs):
        body(*refs[:position], *refs[position + count :])

    extra = {} if grid is None else {"grid": grid}
    if cost is not None:
        extra["cost_estimate"] = pl.CostEstimate(
            flops=int(cost[0]), bytes_accessed=int(cost[1]), transcendentals=0
        )
    if alias is not None:
        extra["input_output_aliases"] = alias
    return pl.pallas_call(
        kernel,
        in_specs=list(in_specs) + [ANY] * count,
        out_specs=out_specs,
        out_shape=out_shape,
        scratch_shapes=list(scratch),
        compiler_params=pltpu.CompilerParams(vmem_limit_bytes=VMEM_BYTES),
        name=name,
        **extra,
    )(*operands, *after)


def half_turn(array):
    width = array.shape[-1]
    half = HEAD_WIDTH // 2
    lane = lax.broadcasted_iota(jnp.int32, array.shape, 1)
    return jnp.where(
        lane % HEAD_WIDTH < half, pltpu.roll(array, width - half, 1), pltpu.roll(array, half, 1)
    )


def spread_heads(array):
    lane = lax.broadcasted_iota(jnp.int32, array.shape, 1)
    first = lane < HEAD_WIDTH
    other = pltpu.roll(array, HEAD_WIDTH, 1)
    zero = jnp.zeros_like(array)
    return [
        [jnp.where(first, array, zero), jnp.where(first, zero, other)],
        [jnp.where(first, other, zero), jnp.where(first, zero, array)],
    ]


def load_blocks(place, blocks, target, sems):
    rows = blocks[0].shape[0]
    copies = []
    for mask, block in enumerate(blocks):
        start = pl.multiple_of((place ^ mask) * rows, rows)
        copies.append(pltpu.make_async_copy(block, target.at[pl.ds(start, rows), :], sems.at[mask]))
    for copy in copies:
        copy.start()
    return copies


def wait_all(copies):
    for copy in copies:
        copy.wait()


def column_of(row_ref, start, size):
    row = jnp.broadcast_to(row_ref[:, start : start + size].astype(wide), (LANES, size))
    return jnp.transpose(row)[:, :1].astype(jnp.int32)


def attend_body(
    place_ref, own, near, far, both, wq_ref, wk_ref, wv_ref, cos_ref, sin_ref, row_ref,
    att_ref, q_ref, k_ref, v_ref, lse_ref, rows_s, kz_s, vz_s, sems,
):
    place = place_ref[0]
    wait_all(load_blocks(place, (own, near, far, both), rows_s, sems))
    length = rows_s.shape[0]
    pairs = wq_ref.shape[1] // LANES
    scale = HEAD_WIDTH**-0.5
    for start in range(0, length, BLOCK):
        at = pl.ds(start, BLOCK)
        rows = rows_s[at, :]
        cos, sin = cos_ref[at, :], sin_ref[at, :]
        query = dot(rows, wq_ref[...], NN)
        for j in range(pairs):
            part = query[:, j * LANES : (j + 1) * LANES]
            turned = (part * cos + half_turn(part) * sin).astype(low)
            q_ref[at, j * LANES : (j + 1) * LANES] = (turned.astype(wide) * scale).astype(low)
        key = dot(rows, wk_ref[...], NN)
        key = (key * cos + half_turn(key) * sin).astype(low)
        k_ref[at, :] = key
        value = dot(rows, wv_ref[...], NN).astype(low)
        v_ref[at, :] = value
        keys, values = spread_heads(key.astype(wide)), spread_heads(value.astype(wide))
        for g in range(2):
            for off in range(2):
                kz_s[2 * g + off, at, :] = keys[g][off].astype(low)
                vz_s[2 * g + off, at, :] = values[g][off].astype(low)
    lane = lax.broadcasted_iota(jnp.int32, (BLOCK, LANES), 1)
    for start in range(0, length, BLOCK):
        at = pl.ds(start, BLOCK)
        first = max(0, start - REACH)
        span = start + BLOCK - first
        keys_at = pl.ds(first, span)
        row_id = lax.broadcasted_iota(jnp.int32, (BLOCK, span), 0) + start
        col_id = lax.broadcasted_iota(jnp.int32, (BLOCK, span), 1) + first
        allowed = (column_of(row_ref, start, BLOCK) == row_ref[:, keys_at]) & (row_id >= col_id)
        bias = jnp.where(allowed, 0.0, NEG)
        stats = jnp.zeros((BLOCK, LANES), wide)
        for j in range(pairs):
            query = q_ref[at, j * LANES : (j + 1) * LANES]
            total = None
            for off in range(2):
                h = 2 * j + off
                slot = 2 * (h // pairs) + off
                scores = dot(query, kz_s[slot, keys_at, :], NT) + bias
                largest = jnp.max(scores, axis=1, keepdims=True)
                shifted = jnp.exp(scores - largest)
                summed = jnp.sum(shifted, axis=1, keepdims=True)
                probs = (shifted * (1.0 / summed)).astype(low)
                part = dot(probs, vz_s[slot, keys_at, :], NN)
                total = part if total is None else total + part
                stats = jnp.where(lane == h, largest + jnp.log(summed), stats)
            att_ref[at, j * LANES : (j + 1) * LANES] = total.astype(low)
        lse_ref[at, :] = stats


def attend(place, blocks, wq, wk, wv, cos, sin, segs, after):
    rows, width = blocks[0].shape
    length = 4 * rows
    return call(
        attend_body,
        (place, *blocks, wq, wk, wv, cos, sin, segs.reshape(1, length)),
        [SMEM] + [ANY] * 4 + [VMEM] * 6,
        [VMEM] * 5,
        [
            Shape((length, wq.shape[1]), low),
            Shape((length, wq.shape[1]), low),
            Shape((length, wk.shape[1]), low),
            Shape((length, wk.shape[1]), low),
            Shape((length, LANES), wide),
        ],
        [
            pltpu.VMEM((length, width), low),
            pltpu.VMEM((4, length, LANES), low),
            pltpu.VMEM((4, length, LANES), low),
            pltpu.SemaphoreType.DMA((4,)),
        ],
        after=after,
        name="attend",
        cost=(15e-6 * 1.1e15, 12e6),
    )


def branch_body(flip, place_ref, att_ref, wo_ref, out_ref):
    rows = out_ref.shape[1]
    core = place_ref[0] % 2
    core = 1 - core if flip else core
    for x in range(2):
        at = pl.ds(pl.multiple_of((2 * x + core) * rows, rows), rows)
        out_ref[x] = dot(att_ref[at, :], wo_ref[...], NN).astype(low)


def branch_half(place, att, wo, flip, after=()):
    rows, width = att.shape[0] // 4, wo.shape[1]
    return call(
        functools.partial(branch_body, flip),
        (place, att, wo),
        [SMEM] + [VMEM] * 2,
        VMEM,
        Shape((2, rows, width), low),
        after=after,
        name="branch",
        cost=(2e9, 4e6),
    )


def attend_back_body(
    place_ref, own, near, far, both, wo_ref, att_ref, q_ref, k_ref, v_ref, lse_ref, cos_ref, sin_ref, row_ref,
    d_lin_ref, rows_s, kz_s, kt_s, vz_s, d_att_s, d_key_s, d_value_s, d_query_s, sems,
):
    place = place_ref[0]
    wait_all(load_blocks(place, (own, near, far, both), rows_s, sems))
    length, q_width = att_ref.shape
    heads = q_width // HEAD_WIDTH
    pairs = heads // 2
    scale = HEAD_WIDTH**-0.5
    lane = lax.broadcasted_iota(jnp.int32, (BLOCK, LANES), 1)
    stats_t = []
    for start in range(0, length, BLOCK):
        at = pl.ds(start, BLOCK)
        d_att = dot(rows_s[at, :], wo_ref[...], NT).astype(low)
        d_att_s[at, :] = d_att
        product = d_att.astype(wide) * att_ref[at, :].astype(wide)
        stats = lse_ref[at, :]
        for h in range(heads):
            part = product[:, (h // 2) * LANES : (h // 2 + 1) * LANES]
            mine = lane // HEAD_WIDTH == h % 2
            inner = jnp.sum(jnp.where(mine, part, 0.0), axis=1, keepdims=True)
            stats = jnp.where(lane == heads + h, inner, stats)
        stats_t.append(jnp.transpose(stats))
        keys, values = spread_heads(k_ref[at, :].astype(wide)), spread_heads(v_ref[at, :].astype(wide))
        for g in range(2):
            for off in range(2):
                kz_s[2 * g + off, at, :] = keys[g][off].astype(low)
                vz_s[2 * g + off, at, :] = values[g][off].astype(low)
                kt_s[2 * g + off, :, at] = jnp.transpose(keys[g][off]).astype(low)
    d_key_s[...] = jnp.zeros_like(d_key_s)
    d_value_s[...] = jnp.zeros_like(d_value_s)
    for i, start in enumerate(range(0, length, BLOCK)):
        at = pl.ds(start, BLOCK)
        first = max(0, start - REACH)
        span = start + BLOCK - first
        keys_at = pl.ds(first, span)
        key_id = lax.broadcasted_iota(jnp.int32, (span, BLOCK), 0) + first
        query_id = lax.broadcasted_iota(jnp.int32, (span, BLOCK), 1) + start
        allowed = (column_of(row_ref, first, span) == row_ref[:, at]) & (query_id >= key_id)
        bias = jnp.where(allowed, 0.0, NEG)
        for j in range(pairs):
            query = q_ref[at, j * LANES : (j + 1) * LANES]
            d_att = d_att_s[at, j * LANES : (j + 1) * LANES]
            total = None
            for off in range(2):
                h = 2 * j + off
                slot = 2 * (h // pairs) + off
                scores = dot(kz_s[slot, keys_at, :], query, NT) + bias
                probs = jnp.exp(scores - stats_t[i][h : h + 1, :])
                d_probs = dot(vz_s[slot, keys_at, :], d_att, NT)
                d_scores = probs * (d_probs - stats_t[i][heads + h : heads + h + 1, :])
                d_scores = d_scores.astype(low)
                d_value_s[slot, keys_at, :] += dot(probs.astype(low), d_att, NN)
                d_key_s[slot, keys_at, :] += dot(d_scores, query, NN)
                part = dot(kt_s[slot, :, keys_at], d_scores, NN)
                total = part if total is None else total + part
            d_query_s[j * LANES : (j + 1) * LANES, at] = total
    for start in range(0, length, BLOCK):
        at = pl.ds(start, BLOCK)
        cos, sin = cos_ref[at, :], sin_ref[at, :]
        for j in range(pairs):
            part = jnp.transpose(d_query_s[j * LANES : (j + 1) * LANES, at]) * scale
            turned = part * cos - half_turn(part) * sin
            d_lin_ref[at, j * LANES : (j + 1) * LANES] = turned.astype(low)
        both_of = []
        for ref in (d_key_s, d_value_s):
            first_head = ref[0, at, :] + pltpu.roll(ref[1, at, :], HEAD_WIDTH, 1)
            second_head = ref[3, at, :] + pltpu.roll(ref[2, at, :], HEAD_WIDTH, 1)
            both_of.append(jnp.where(lane < HEAD_WIDTH, first_head, second_head))
        d_key, d_value = both_of
        d_lin_ref[at, q_width : q_width + LANES] = (d_key * cos - half_turn(d_key) * sin).astype(low)
        d_lin_ref[at, q_width + LANES :] = d_value.astype(low)


def attend_back(place, blocks, wo, att, q, k, v, lse, cos, sin, segs, after):
    rows, width = blocks[0].shape
    length, q_width = att.shape
    return call(
        attend_back_body,
        (place, *blocks, wo, att, q, k, v, lse, cos, sin, segs.reshape(1, length)),
        [SMEM] + [ANY] * 4 + [VMEM] * 9,
        VMEM,
        Shape((length, q_width + 2 * LANES), low),
        [
            pltpu.VMEM((length, width), low),
            pltpu.VMEM((4, length, LANES), low),
            pltpu.VMEM((4, LANES, length), low),
            pltpu.VMEM((4, length, LANES), low),
            pltpu.VMEM((length, q_width), low),
            pltpu.VMEM((4, length, LANES), wide),
            pltpu.VMEM((4, length, LANES), wide),
            pltpu.VMEM((q_width, length), wide),
            pltpu.SemaphoreType.DMA((4,)),
        ],
        after=after,
        name="attend_back",
        cost=(15e-6 * 1.1e15, 12e6),
    )


def split_add_body(place_ref, mine_ref, got_ref, kept_ref, sent_ref):
    far = place_ref[0] // 2
    kept_ref[...] = (mine_ref[far].astype(wide) + got_ref[far].astype(wide)).astype(low)
    sent_ref[...] = (mine_ref[1 - far].astype(wide) + got_ref[1 - far].astype(wide)).astype(low)


def tensor_scatter(place, mine, other, after):
    rows, width = mine.shape[1:]
    got = swap(other, "tensor", 1)
    kept, sent = call(
        split_add_body,
        (place, mine, got),
        [SMEM, VMEM, VMEM],
        [VMEM, VMEM],
        [Shape((rows, width), low)] * 2,
        after=after,
        name="split_add",
        cost=(1e9, 6e6),
    )
    return kept, swap(sent, "tensor", 2)


def expert_body(pieces, cuts, local, *refs):
    rows_refs = refs[:pieces]
    up_refs = refs[pieces : 2 * pieces]
    sel_ref, router_ref, gate_ref, up_w_ref, down_ref = refs[2 * pieces : 2 * pieces + 5]
    outs = refs[2 * pieces + 5 :]
    d_rows_refs, mixed_refs = outs[:pieces], outs[pieces : 2 * pieces]
    hidden_ref, d_gate_ref, d_up_ref = outs[2 * pieces : 2 * pieces + 3]
    rows_s, ups_s, d_rows_s, mixed_s, gates_s, d_gates_s, sems = outs[2 * pieces + 3 :]
    step = pl.program_id(0)
    width = rows_s.shape[1]

    @pl.when(step == 0)
    def _():
        copies = []
        for side, (sources, target) in enumerate(((rows_refs, rows_s), (up_refs, ups_s))):
            start = 0
            for i, source in enumerate(sources):
                size = source.shape[0]
                copies.append(
                    pltpu.make_async_copy(
                        source, target.at[pl.ds(start, size), :], sems.at[side * pieces + i]
                    )
                )
                start += size
        for copy in copies:
            copy.start()
        wait_all(copies)
        chosen = ups_s[:, width:] > 0.0
        logits = jnp.where(chosen, dot(rows_s[...], router_ref[...], NN), NEG)
        largest = jnp.max(logits, axis=1, keepdims=True)
        shifted = jnp.where(chosen, jnp.exp(logits - largest), 0.0)
        gates_s[...] = shifted / jnp.sum(shifted, axis=1, keepdims=True)
        d_gates_s[...] = jnp.zeros_like(d_gates_s)

    expert = step // cuts
    pick = sel_ref[0:1, :]
    for e in range(1, local):
        pick = jnp.where(expert == e, sel_ref[e : e + 1, :], pick)
    gate = jnp.sum(gates_s[...] * pick, axis=1, keepdims=True)
    rows = rows_s[...]
    ups = ups_s[:, :width]
    gate_w, up_w, down_w = gate_ref[0], up_w_ref[0], down_ref[0]
    gate_pre = dot(rows, gate_w, NN)
    up_pre = dot(rows, up_w, NN)
    d_act = dot(ups, down_w, NT)
    sig = 1.0 / (1.0 + jnp.exp(-gate_pre))
    act = gate_pre * sig
    hidden = act * up_pre
    d_gates_s[...] += jnp.sum(hidden * d_act, axis=1, keepdims=True) * pick
    hidden = (gate * hidden).astype(low)
    d_act = gate * d_act
    d_gate = (d_act * up_pre * sig * (1.0 + gate_pre * (1.0 - sig))).astype(low)
    d_up = (d_act * act).astype(low)
    hidden_ref[...] = hidden
    d_gate_ref[...] = d_gate
    d_up_ref[...] = d_up
    d_rows = dot(d_gate, gate_w, NT) + dot(d_up, up_w, NT)
    mixed = dot(hidden, down_w, NN)

    @pl.when(step == 0)
    def _():
        d_rows_s[...] = d_rows
        mixed_s[...] = mixed

    @pl.when(step > 0)
    def _():
        d_rows_s[...] += d_rows
        mixed_s[...] += mixed

    @pl.when(step == pl.num_programs(0) - 1)
    def _():
        lane = lax.broadcasted_iota(jnp.int32, d_gates_s.shape, 1)
        d_gates = d_gates_s[...]
        d_gates = jnp.where(lane < LANES // 2, d_gates, pltpu.roll(d_gates, LANES // 2, 1))
        rounded = d_gates.astype(low).astype(wide)
        d_gates = jnp.where(lane < LANES // 2, rounded, d_gates - rounded).astype(low)
        start = 0
        for d_rows_ref, mixed_ref in zip(d_rows_refs, mixed_refs):
            size = d_rows_ref.shape[0]
            d_rows_ref[:, :width] = d_rows_s[start : start + size, :].astype(low)
            d_rows_ref[:, width:] = d_gates[start : start + size, :]
            mixed_ref[...] = mixed_s[start : start + size, :].astype(low)
            start += size


def expert_block(rows_list, ups_list, sel, w_router, w_gate, w_up, w_down, after=()):
    pieces = len(rows_list)
    sizes = [rows.shape[0] for rows in rows_list]
    rows = sum(sizes)
    local, width, ff = w_gate.shape
    cut = min(512, ff)
    cuts = ff // cut
    whole = lambda shape: pl.BlockSpec(shape, lambda j: (0,) * len(shape))
    across = pl.BlockSpec((1, width, cut), lambda j: (j // cuts, 0, j % cuts))
    tall = pl.BlockSpec((1, cut, width), lambda j: (j // cuts, j % cuts, 0))
    part = pl.BlockSpec((rows, cut), lambda j: (0, j))
    outs = call(
        functools.partial(expert_body, pieces, cuts, local),
        (*rows_list, *ups_list, sel, w_router, w_gate, w_up, w_down),
        [ANY] * (2 * pieces) + [whole((local, LANES)), whole((width, LANES)), across, across, tall],
        [whole((size, width + LANES)) for size in sizes]
        + [whole((size, width)) for size in sizes]
        + [part, part, part],
        [Shape((size, width + LANES), low) for size in sizes]
        + [Shape((size, width), low) for size in sizes]
        + [Shape((rows, local * ff), low)] * 3,
        [
            pltpu.VMEM((rows, width), low),
            pltpu.VMEM((rows, width + LANES), low),
            pltpu.VMEM((rows, width), wide),
            pltpu.VMEM((rows, width), wide),
            pltpu.VMEM((rows, LANES), wide),
            pltpu.VMEM((rows, LANES), wide),
            pltpu.SemaphoreType.DMA((2 * pieces,)),
        ],
        grid=(local * cuts,),
        after=after,
        name="experts",
        cost=(19 * rows * width * local * ff, 6 * local * width * ff + 8 * rows * width),
    )
    return outs[:pieces], outs[pieces : 2 * pieces], outs[2 * pieces :]


def outer_body(pieces, seconds, split, *refs):
    first_refs = refs[:pieces]
    second_refs = refs[pieces : pieces + seconds]
    out_ref, first_s, second_s, first_sems, second_sems = refs[pieces + seconds :]
    step = pl.program_id(0)
    cut = first_s.shape[2]
    width = second_s.shape[1]

    def load(at, slot):
        copies, start = [], 0
        for i, ref in enumerate(first_refs):
            size = ref.shape[0]
            copies.append(
                pltpu.make_async_copy(
                    ref.at[:, pl.ds(pl.multiple_of(at * cut, cut), cut)],
                    first_s.at[slot, pl.ds(start, size), :],
                    first_sems.at[slot, i],
                )
            )
            start += size
        return copies

    slot = step % 2

    @pl.when(step == 0)
    def _():
        for copy in load(0, 0):
            copy.start()
        copies, start = [], 0
        for i, ref in enumerate(second_refs):
            size = ref.shape[0]
            copies.append(
                pltpu.make_async_copy(
                    ref.at[:, pl.ds(0, width)], second_s.at[pl.ds(start, size), :], second_sems.at[i]
                )
            )
            start += size
        for copy in copies:
            copy.start()
        wait_all(copies)

    @pl.when(step + 1 < pl.num_programs(0))
    def _():
        for copy in load(step + 1, 1 - slot):
            copy.start()

    wait_all(load(step, slot))
    product = dot(first_s[slot], second_s[...], TN).astype(low)
    if split == 1:
        out_ref[0] = product
    else:
        part = width // split
        for e in range(split):
            out_ref[e] = product[:, e * part : (e + 1) * part]


def outer_products(first, second, first_width, second_width, split, after=()):
    cut = 512
    steps = first_width // cut
    rows = sum(piece.shape[0] for piece in first)
    if split == 1:
        out_shape = Shape((steps, cut, second_width), low)
        out_spec = pl.BlockSpec((1, cut, second_width), lambda i: (i, 0, 0))
    else:
        part = second_width // split
        out_shape = Shape((split, first_width, part), low)
        out_spec = pl.BlockSpec((split, cut, part), lambda i: (0, i, 0))
    return call(
        functools.partial(outer_body, len(first), len(second), split),
        (*first, *second),
        [ANY] * (len(first) + len(second)),
        out_spec,
        out_shape,
        [
            pltpu.VMEM((2, rows, cut), low),
            pltpu.VMEM((rows, second_width), low),
            pltpu.SemaphoreType.DMA((2, len(first))),
            pltpu.SemaphoreType.DMA((len(second),)),
        ],
        grid=(steps,),
        after=after,
        name="outer_products",
        cost=(3.5 * rows * first_width * second_width, 12e6),
    )


def head_grads_body(count, place_ref, ids_ref, *refs):
    rows_refs, d_refs = refs[:4], refs[4:8]
    att_ref, d_lin_ref, wq_ref, wk_ref, wv_ref, gain_ref = refs[8:14]
    outs = refs[14 : 14 + count + 1]
    gain_out, rows_s, d_s, flat_s, sems = refs[15 + count :]
    place = place_ref[0]
    copies = load_blocks(place, rows_refs, rows_s, sems)
    start = pl.multiple_of
    rows = rows_refs[0].shape[0]
    more = []
    for mask, block in enumerate(d_refs):
        at = pl.ds(start((place ^ mask) * rows, rows), rows)
        more.append(pltpu.make_async_copy(block, d_s.at[at, :], sems.at[4 + mask]))
    for copy in more:
        copy.start()
    wait_all(copies)
    q_width, kv_width = wq_ref.shape[1], wk_ref.shape[1]
    lin_width = d_lin_ref.shape[1]
    width = rows_s.shape[1]
    for at in range(0, width, 512):
        here = pl.ds(at, 512)
        grads = dot(rows_s[:, here], d_lin_ref[...], TN)
        for c in range(0, lin_width, LANES):
            flat_s[c // LANES * width + at : c // LANES * width + at + 512, :] = grads[:, c : c + LANES].astype(low)
        inner = jnp.sum(wq_ref[here, :].astype(wide) * grads[:, :q_width], axis=1, keepdims=True)
        inner += jnp.sum(
            wk_ref[here, :].astype(wide) * grads[:, q_width : q_width + kv_width], axis=1, keepdims=True
        )
        inner += jnp.sum(
            wv_ref[here, :].astype(wide) * grads[:, q_width + kv_width :], axis=1, keepdims=True
        )
        inner = jnp.transpose(jnp.broadcast_to(inner, (512, LANES)))[:1]
        gain_out[:, here] = inner / gain_ref[:, here]
    wait_all(more)
    base = lin_width // LANES * width
    for at in range(0, width, 512):
        grads = dot(att_ref[...], d_s[:, at : at + 512], TN).astype(low)
        for c in range(0, 512, LANES):
            row = base + (at + c) // LANES * q_width
            flat_s[row : row + q_width, :] = grads[:, c : c + LANES]
    for o, ref in enumerate(outs):
        size = ref.shape[0]
        part = flat_s.shape[0] // count
        if o < count // 2:
            at = ids_ref[o] * part
        elif o > count // 2 + 1:
            at = ids_ref[o - 1] * part
        else:
            at = ids_ref[count // 2] * part + (o - count // 2) * size
        ref[...] = flat_s[pl.ds(start(at, size), size), :]


def head_grads(place, ids, rows_blocks, d_blocks, att, d_lin, wq, wk, wv, gain):
    count = lax.axis_size("dp")
    rows, width = rows_blocks[0].shape
    length, q_width = att.shape
    flat = width * (d_lin.shape[1] + q_width) // LANES
    part = flat // count
    sizes = [part] * (count // 2) + [part // 2] * 2 + [part] * (count // 2 - 1)
    outs = call(
        functools.partial(head_grads_body, count),
        (place, ids, *rows_blocks, *d_blocks, att, d_lin, wq, wk, wv, gain),
        [SMEM, SMEM] + [ANY] * 8 + [VMEM] * 6,
        [VMEM] * (count + 2),
        [Shape((size, LANES), low) for size in sizes] + [Shape((1, width), wide)],
        [
            pltpu.VMEM((length, width), low),
            pltpu.VMEM((length, width), low),
            pltpu.VMEM((flat, LANES), low),
            pltpu.SemaphoreType.DMA((8,)),
        ],
        name="head_grads",
        cost=(6e-6 * 1.1e15, 12e6),
    )
    parts = list(outs[: count // 2]) + [(outs[count // 2], outs[count // 2 + 1])] + list(outs[count // 2 + 2 : -1])
    return parts, outs[-1]


def head_place_body(count, ids_ref, *refs):
    blocks = refs[: count + 1]
    grad_q, grad_k, grad_v, grad_o, flat_s = refs[count + 1 :]
    width, q_width = grad_q.shape
    part = flat_s.shape[0] // count
    for o, ref in enumerate(blocks):
        size = ref.shape[0]
        if o < count // 2:
            at = ids_ref[o] * part
        elif o > count // 2 + 1:
            at = ids_ref[o - 1] * part
        else:
            at = ids_ref[count // 2] * part + (o - count // 2) * size
        flat_s[pl.ds(pl.multiple_of(at, size), size), :] = ref[...]
    row = 0
    for ref in (grad_q, grad_k, grad_v, grad_o):
        rows, columns = ref.shape
        for c in range(0, columns, LANES):
            ref[:, c : c + LANES] = flat_s[row : row + rows, :].astype(wide)
            row += rows


def head_place(ids, blocks, width, q_width, kv_width):
    count = lax.axis_size("dp")
    return call(
        functools.partial(head_place_body, count),
        (ids, *blocks),
        [SMEM] + [VMEM] * (count + 1),
        [VMEM] * 4,
        [
            Shape((width, q_width), wide),
            Shape((width, kv_width), wide),
            Shape((width, kv_width), wide),
            Shape((q_width, width), wide),
        ],
        [pltpu.VMEM((width * (2 * q_width + 2 * kv_width) // LANES, LANES), low)],
        name="head_place",
        cost=(1e9, 8e6),
    )


def widen_body(in_ref, out_ref):
    out_ref[...] = in_ref[...].astype(wide)


def widen(array, after):
    count, rows, columns = array.shape
    spec = pl.BlockSpec((1, 256, columns), lambda i: (i * 256 // rows, i % (rows // 256), 0))
    return call(
        widen_body, (array,), [spec], spec, Shape(array.shape, wide), grid=(count * rows // 256,),
        after=after, name="widen", cost=(1e8, 10e6),
    )


def lin_back_body(place_ref, d_lin_ref, wq_ref, wk_ref, wv_ref, mine_ref, other_ref):
    rows = mine_ref.shape[1]
    core = place_ref[0] % 2
    q_width, kv_width = wq_ref.shape[1], wk_ref.shape[1]
    for x in range(2):
        for ref, c in ((other_ref, 1 - core), (mine_ref, core)):
            at = pl.ds(pl.multiple_of((2 * x + c) * rows, rows), rows)
            total = dot(d_lin_ref[at, :q_width], wq_ref[...], NT)
            total += dot(d_lin_ref[at, q_width : q_width + kv_width], wk_ref[...], NT)
            total += dot(d_lin_ref[at, q_width + kv_width :], wv_ref[...], NT)
            ref[x] = total.astype(low)


def lin_back(place, d_lin, wq, wk, wv, after):
    rows, width = d_lin.shape[0] // 4, wq.shape[0]
    return call(
        lin_back_body,
        (place, d_lin, wq, wk, wv),
        [SMEM] + [VMEM] * 4,
        [VMEM] * 2,
        [Shape((2, rows, width), low)] * 2,
        after=after,
        name="lin_back",
        cost=(4e-6 * 1.1e15, 9e6),
    )


def first_norm_body(tokens_ref, gain_ref, normed_ref):
    inputs = tokens_ref[...].astype(wide)
    inverse = lax.rsqrt(jnp.mean(inputs * inputs, axis=1, keepdims=True) + EPS)
    normed_ref[...] = (inputs * inverse * gain_ref[...]).astype(low)


def second_norm_body(tokens_ref, kept_ref, got_ref, gain_ref, residual_ref, normed_ref):
    residual = tokens_ref[...].astype(wide) + (kept_ref[...].astype(wide) + got_ref[...].astype(wide))
    inverse = lax.rsqrt(jnp.mean(residual * residual, axis=1, keepdims=True) + EPS)
    residual_ref[...] = residual
    normed_ref[...] = (residual * inverse * gain_ref[...]).astype(low)


def middle_body(
    own_ref, up_ref, down_ref, residual_ref, normed_ref, ups_ref, router_ref, gain_ref, passed_ref,
    d_residual_ref, d_low_ref, gain_out, router_out, passed_out,
):
    del passed_ref, passed_out
    width = residual_ref.shape[1]
    total = own_ref[...].astype(wide) + up_ref[...].astype(wide) + down_ref[...].astype(wide)
    d_gates = total[:, width:]
    d_gates = d_gates + pltpu.roll(d_gates, LANES // 2, 1)
    lane = lax.broadcasted_iota(jnp.int32, d_gates.shape, 1)
    chosen = ups_ref[:, width:] > 0.0
    normed = normed_ref[...]
    logits = jnp.where(chosen, dot(normed, router_ref[...], NN), NEG)
    largest = jnp.max(logits, axis=1, keepdims=True)
    shifted = jnp.where(chosen, jnp.exp(logits - largest), 0.0)
    gates = shifted / jnp.sum(shifted, axis=1, keepdims=True)
    inner = jnp.sum(gates * d_gates, axis=1, keepdims=True)
    d_logits = (gates * (d_gates - inner)).astype(low)
    router_out[...] = dot(d_logits, normed, TN)[: router_out.shape[0]]
    d_normed = total[:, :width] + dot(d_logits, router_ref[...], NT)
    residual = residual_ref[...]
    inverse = lax.rsqrt(jnp.mean(residual * residual, axis=1, keepdims=True) + EPS)
    scaled = d_normed * gain_ref[...]
    mean = jnp.mean(scaled * residual, axis=1, keepdims=True)
    upstream = ups_ref[:, :width].astype(wide)
    d_residual = upstream + inverse * scaled - residual * (inverse * inverse * inverse * mean)
    gain_out[...] = jnp.sum(d_normed * residual * inverse, axis=0, keepdims=True)
    d_residual_ref[...] = d_residual
    d_low_ref[...] = d_residual.astype(low)


def last_body(tokens_ref, kept_ref, got_ref, d_residual_ref, gain_ref, out_ref):
    inputs = tokens_ref[...].astype(wide)
    inverse = lax.rsqrt(jnp.mean(inputs * inputs, axis=1, keepdims=True) + EPS)
    scaled = (kept_ref[...].astype(wide) + got_ref[...].astype(wide)) * gain_ref[...]
    mean = jnp.mean(scaled * inputs, axis=1, keepdims=True)
    d_inputs = inverse * scaled - inputs * (inverse * inverse * inverse * mean)
    out_ref[...] = (d_inputs + d_residual_ref[...]).astype(low)


def on_device(
    tokens,
    gain_attn,
    query_weight,
    key_weight,
    value_weight,
    w_output,
    gain_ffn,
    w_router,
    w_gate,
    w_up,
    w_down,
    segments,
    routes,
    cotangent,
):
    rows_dev, width = tokens.shape
    data_count = lax.axis_size("dp")
    half_count = data_count // 2
    local_experts, _, ff = w_gate.shape
    expert_count = local_experts * data_count
    q_width, kv_width = query_weight.shape[1], key_weight.shape[1]
    place = lax.axis_index("tensor").astype(jnp.int32).reshape(1)
    ids = ring_places()
    cos, sin = rope_tables(segments.shape[1])
    gain_one, gain_two = gain_attn.reshape(1, width), gain_ffn.reshape(1, width)
    lanes = jnp.arange(LANES, dtype=jnp.int32)
    own_experts = lax.axis_index("dp") * local_experts + jnp.arange(local_experts, dtype=jnp.int32)
    sel = (own_experts[:, None] == lanes[None, :]).astype(wide)
    router = jnp.pad(w_router, ((0, 0), (0, LANES - expert_count)))
    chosen = jnp.any(routes[:, :, None] == lanes[None, None, :], axis=1).astype(low)
    ups = jnp.concatenate([cotangent, chosen], axis=1)

    normed_one = call(
        first_norm_body, (tokens, gain_one), [VMEM] * 2, VMEM, Shape((rows_dev, width), low),
        name="first_norm", cost=(1e9, 2e6),
    )
    ups_below, ups_above, ups_far = ring_gather(ups)
    rows_blocks = tensor_blocks(normed_one)
    att, q, k, v, lse = attend(
        place, rows_blocks, query_weight, key_weight, value_weight, cos, sin, segments,
        after=(ups_below[0], ups_above[0]),
    )
    other = branch_half(place, att, w_output, True)
    mine = branch_half(place, att, w_output, False, after=(ups_below[1], ups_above[1]))
    kept, got = tensor_scatter(place, mine, other, after=())
    residual, normed_two = call(
        second_norm_body, (tokens, kept, got, gain_two), [VMEM] * 4, [VMEM] * 2,
        [Shape((rows_dev, width), wide), Shape((rows_dev, width), low)],
        after=(ups_below[2], ups_above[2]), name="second_norm", cost=(1e9, 4e6),
    )
    rows_below, rows_above, rows_far = ring_gather(normed_two)
    groups = [((normed_two,), (ups,))]
    for k_ in range(half_count - 1):
        groups.append(((rows_below[k_], rows_above[k_]), (ups_below[k_], ups_above[k_])))
    groups.append((rows_far, ups_far))
    done = []
    for rows, up in groups:
        after = () if not done else (done[-1][2][0],)
        if len(done) == 1:
            after += tuple(ups_far)
        done.append(expert_block(rows, up, sel, router, w_gate, w_up, w_down, after))
    d_rows_up, d_rows_down = ring_scatter(
        [outs[0][0] for outs in done[1:-1]], [outs[0][1] for outs in done[1:-1]], done[-1][0]
    )
    far_mixed = list(done[-1][1])
    d_residual, d_low, gain_ffn_part, router_part, far_mixed[0] = call(
        middle_body,
        (done[0][0][0], d_rows_up, d_rows_down, residual, normed_two, ups, router, gain_two, far_mixed[0]),
        [VMEM] * 8 + [ANY],
        [VMEM] * 4 + [ANY],
        [
            Shape((rows_dev, width), wide),
            Shape((rows_dev, width), low),
            Shape((1, width), wide),
            Shape((expert_count, width), wide),
            Shape(far_mixed[0].shape, low),
        ],
        name="middle", cost=(4e-6 * 1.1e15, 4e6), alias={8: 4},
    )
    rows_all = [piece for rows, _ in groups for piece in rows]
    ups_all = [piece for _, up in groups for piece in up]
    hidden_all, d_gate_all, d_up_all = ([outs[2][i] for outs in done] for i in range(3))
    inner = local_experts * ff
    grad_down = outer_products(hidden_all, ups_all, inner, width, 1).reshape(local_experts, ff, width)
    grad_gate = outer_products(rows_all, d_gate_all, width, inner, local_experts)
    grad_up = outer_products(rows_all, d_up_all, width, inner, local_experts)
    grad_gate, grad_up, grad_down = (
        lax.psum(grad, "tensor") for grad in (grad_gate, grad_up, grad_down)
    )
    mixed_up, mixed_down = ring_scatter(
        [outs[1][0] for outs in done[1:-1]], [outs[1][1] for outs in done[1:-1]], far_mixed
    )
    mixed = (
        residual + done[0][1][0].astype(wide) + mixed_up.astype(wide) + mixed_down.astype(wide)
    ).astype(low)

    d_blocks = tensor_blocks(d_low)
    d_lin = attend_back(place, d_blocks, w_output, att, q, k, v, lse, cos, sin, segments, after=())
    parts, gain_attn_part = head_grads(
        place, ids, rows_blocks, d_blocks, att, d_lin, query_weight, key_weight, value_weight, gain_one
    )
    mine, other = lin_back(place, d_lin, query_weight, key_weight, value_weight, after=())
    kept, got = tensor_scatter(place, mine, other, after=())
    grad_tokens = call(
        last_body, (tokens, kept, got, d_residual, gain_one), [VMEM] * 5, VMEM,
        Shape((rows_dev, width), low), name="last", cost=(1e9, 4e6),
    )
    up, down = ring_scatter(
        [parts[data_count - 1 - i] for i in range(half_count - 1)],
        [parts[1 + i] for i in range(half_count - 1)],
        parts[half_count],
    )
    total = (parts[0].astype(wide) + up.astype(wide) + down.astype(wide)).astype(low)
    below, above, far = ring_gather(total)
    grad_q, grad_k, grad_v, grad_o = head_place(
        ids, [total] + above + list(far) + below[::-1], width, q_width, kv_width
    )
    grad_gate = widen(grad_gate, (below[0], above[0]))
    grad_up = widen(grad_up, (below[0], above[0]))
    grad_down = widen(grad_down, (below[0], above[0]))
    small = jnp.concatenate([gain_ffn_part, gain_attn_part, router_part], axis=0)
    small = cube_sum(small, ("tensor", "dp"))
    return (
        mixed,
        grad_tokens,
        small[1],
        grad_q,
        grad_k,
        grad_v,
        grad_o,
        small[0],
        small[2:].T,
        grad_gate,
        grad_up,
        grad_down,
    )


def solution(mesh):
    in_specs = (
        P(("dp", "tensor"), None),
        P(),
        P(None, "tensor"),
        P(None, "tensor"),
        P(None, "tensor"),
        P("tensor", None),
        P(),
        P(),
        P("dp", None, None),
        P("dp", None, None),
        P("dp", None, None),
        P("dp", None),
        P(("dp", "tensor"), None),
        P(("dp", "tensor"), None),
    )
    out_specs = (
        P(("dp", "tensor"), None),
        P(("dp", "tensor"), None),
        P(),
        P(None, "tensor"),
        P(None, "tensor"),
        P(None, "tensor"),
        P("tensor", None),
        P(),
        P(),
        P("dp", None, None),
        P("dp", None, None),
        P("dp", None, None),
    )
    return jax.shard_map(
        on_device, mesh=mesh, in_specs=in_specs, out_specs=out_specs, check_vma=False
    )
```

time: 1370 us -> 557 us (0.41)
  waiting for transfers between devices: 884 us -> 222 us
  Pallas kernels: 0 us -> 217 us
  matrix products: 187 us -> 0 us
  local copies, waits for them, and re-layouts: 110 us -> 19 us
  other arithmetic: 102 us -> 11.8 us
  blocking collectives: 48.6 us -> 0 us
  starting transfers between devices: 21.3 us -> 60.5 us
    all_to_all x4 -> x0, waiting for transfers between devices: 568 us -> none  [the longest x1 151 us: on_device(): lax.all_to_all(d_send, 'dp', split_axis=0, concat_axis=0, tiled=True)]
    pallas_call x0 -> x24, Pallas kernels: none -> 217 us  [call(): pl.pallas_call(kernel, in_specs=list(in_specs) + [ANY] * count, out_specs...]
    ppermute x0 -> x63, waiting for transfers between devices: none -> 193 us  [the longest x48 150 us: ring_send(): lax.ppermute(array, 'dp', [(order[i], order[(i + step) % count]) for i in...]
    dot_general x36 -> x0, matrix products: 187 us -> none  [the longest x2 17.6 us: attend_back(): jnp.einsum('qkgd,tkd->kgqt', d_block, value_seq, preferred_element_type=j...]
    psum x2 -> x1, waiting for transfers between devices: 209 us -> 29 us  [on_device(): lax.psum(grad, 'tensor')]
    reduce_scatter x2 -> x0, waiting for transfers between devices: 79.8 us -> none  [the longest x1 49.1 us: on_device(): lax.psum_scatter(jnp.dot(lax.slice_in_dim(attended_flat, 0, rows_dev * la...]
    gather x4 -> x0, local copies, waits for them, and re-layouts: 73.7 us -> none  [the longest x1 20 us: on_device(): jnp.concatenate([d_expert, zero_row], axis=0)[pair_of_slot]]
    ppermute x0 -> x63, starting transfers between devices: none -> 60.5 us  [the longest x48 50.9 us: ring_send(): lax.ppermute(array, 'dp', [(order[i], order[(i + step) % count]) for i in...]
  transfers between devices with their start and end apart: 10 -> 64, of which waited for: 9 -> 28; matrix products, arithmetic and copies ran while one was open for 19% -> 3% of each run, Pallas kernels for 0% -> 32%
where the time goes in v1:
time: 557 us; the launch traced here: 546 us
  waiting for transfers between devices  222 us (40%)
  Pallas kernels  217 us (39%)
  starting transfers between devices  60.5 us (11%)
  local copies, waits for them, and re-layouts  19 us (3%)
  between operations  15.4 us (3%)
  other arithmetic  11.8 us (2%)
    pallas_call x24, Pallas kernels, call(): pl.pallas_call(kernel, in_specs=list(in_specs) + [ANY] * count, out_specs...  217 us
    ppermute x48, waiting for transfers between devices, ring_send(): lax.ppermute(array, 'dp', [(order[i], order[(i + step) % count]) for i in...  150 us
    ppermute x48, starting transfers between devices, ring_send(): lax.ppermute(array, 'dp', [(order[i], order[(i + step) % count]) for i in...  50.9 us
    ppermute x15, waiting for transfers between devices, swap(): lax.ppermute(array, axis, [(i, i ^ mask) for i in range(lax.axis_size(axi...  43.2 us
    psum x1, waiting for transfers between devices, on_device(): lax.psum(grad, 'tensor')  29 us
    unnamed x170, local copies, waits for them, and re-layouts  11.8 us
  transfers between devices with their start and end apart: 64, of which 28 were waited for; matrix products, arithmetic and copies ran while one was open for 3% of the time, Pallas kernels for 32%

profile of v1, /device:TPU:0, one launch (start us, length us, event | category | flops | bytes accessed | tf_op | source)
XLA Modules:
  0.0 546.3 jit_solution(12196633915898563162)
XLA Ops:
  9.7 3.0 collective-permute-start.1
  13.4 1.6 collective-permute-start.3
  15.4 14.9 %collective-permute-done.1.refs_3_.refs_4_ = bf16[256,1536]{1,0:T(8,128)(2,1)} collective-permute-done((bf16[256,1536]{1,0:T(8,128)(2,1)S(1)}, bf16[256,1536]{1,0:T(8,128)(2,1)}, u32[]{:S(2)}, u32[]{:S(2)}) %collective-permute-start.1) | collective-permute-done | bytes 786464 | tf_op jit(solution)/shard_map/ppermute | solution.py:99
  30.3 3.5 collective-permute-done.3.refs_11_.refs_2_.refs_6_
  35.3 16.5 %attend.1 = (bf16[1024,384]{1,0:T(8,128)(2,1)}, bf16[1024,384]{1,0:T(8,128)(2,1)}, bf16[1024,128]{1,0:T(8,128)(2,1)S(1)}, bf16[1024,128]{1,0:T(8,128)(2,1)S(1)}, f32[1024,128]{1,0:T(8,128)S(1)}) custom-call(s32[1]{0:T(128)} %bitcast.refs_0_, bf16[256,1536]{1,0:T(8,128)(2,1)} %copy-done.10, bf16[256,1536]{1,0:T(8,128)(2,1)} %collective-permute-done.refs_2_.refs_3_, ...), custom_call_target="tpu_custom_call" | custom-call | flops 16499999744 | bytes 12000000 | tf_op jit(solution)/shard_map/attend/pallas_call | solution.py:130
  54.6 2.3 branch.3
  56.9 1.6 collective-permute-start.5
  59.0 19.3 %collective-permute-done.5.refs_3_.refs_2_.refs_8_ = bf16[256,1664]{1,0:T(8,128)(2,1)S(1)} collective-permute-done((bf16[256,1664]{1,0:T(8,128)(2,1)S(1)}, bf16[256,1664]{1,0:T(8,128)(2,1)S(1)}, u32[]{:S(2)}, u32[]{:S(2)}) %collective-permute-start.5) | collective-permute-done | bytes 852000 | tf_op jit(solution)/shard_map/ppermute | solution.py:49
  80.3 3.4 branch.2.refs_1_
  84.9 2.2 split_add.2
  88.6 10.3 %collective-permute-done.9.refs_4_.refs_2_.refs_10_ = bf16[256,1664]{1,0:T(8,128)(2,1)S(1)} collective-permute-done((bf16[256,1664]{1,0:T(8,128)(2,1)S(1)}, bf16[256,1664]{1,0:T(8,128)(2,1)S(1)}, u32[]{:S(2)}, u32[]{:S(2)}) %collective-permute-start.9) | collective-permute-done | bytes 852000 | tf_op jit(solution)/shard_map/ppermute | solution.py:49
  98.9 1.6 collective-permute-done.10.refs_5_.refs_3_.refs_11_
  100.5 6.2 %collective-permute-done.8.refs_2_ = bf16[256,1536]{1,0:T(8,128)(2,1)} collective-permute-done((bf16[256,1536]{1,0:T(8,128)(2,1)S(1)}, bf16[256,1536]{1,0:T(8,128)(2,1)}, u32[]{:S(2)}, u32[]{:S(2)}) %collective-permute-start.8) | collective-permute-done | bytes 786464 | tf_op jit(solution)/shard_map/ppermute | solution.py:99
  106.7 3.0 second_norm.1
  109.8 1.6 collective-permute-start.11
  113.2 1.6 collective-permute-start.19
  116.4 12.7 %experts.5 = (bf16[256,1664]{1,0:T(8,128)(2,1)}, bf16[256,1536]{1,0:T(8,128)(2,1)}, bf16[256,1024]{1,0:T(8,128)(2,1)S(1)}, bf16[256,1024]{1,0:T(8,128)(2,1)S(1)}, bf16[256,1024]{1,0:T(8,128)(2,1)S(1)}) custom-call(bf16[256,1536]{1,0:T(8,128)(2,1)} %copy-done.11, bf16[256,1664]{1,0:T(8,128)(2,1)} %copy-done.57, ...), custom_call_target="tpu_custom_call" | custom-call | flops 7650410496 | bytes 12582912 | tf_op jit(solution)/shard_map/experts/pallas_call | solution.py:130
  132.6 6.8 %collective-permute-done.19.refs_10_.refs_2_.refs_12_ = bf16[128,1664]{1,0:T(8,128)(2,1)S(1)} collective-permute-done((bf16[128,1664]{1,0:T(8,128)(2,1)S(1)}, bf16[128,1664]{1,0:T(8,128)(2,1)S(1)}, u32[]{:S(2)}, u32[]{:S(2)}) %collective-permute-start.19) | collective-permute-done | bytes 426016 | tf_op jit(solution)/shard_map/ppermute | solution.py:49
  140.9 20.4 %experts.6 = (bf16[256,1664]{1,0:T(8,128)(2,1)}, bf16[256,1664]{1,0:T(8,128)(2,1)}, bf16[256,1536]{1,0:T(8,128)(2,1)}, bf16[256,1536]{1,0:T(8,128)(2,1)}, bf16[5...) custom-call(bf16[256,1536]{1,0:T(8,128)(2,1)} %collective-permute-done.11.refs_0_.refs_1_, ...), custom_call_target="tpu_custom_call" | custom-call | flops 15300820992 | bytes 15728640 | tf_op jit(solution)/shard_map/experts/pallas_call | solution.py:130
  161.4 1.6 collective-permute-start.13
  164.0 19.6 %experts.7 = (bf16[256,1664]{1,0:T(8,128)(2,1)}, bf16[256,1664]{1,0:T(8,128)(2,1)}, bf16[256,1536]{1,0:T(8,128)(2,1)S(1)}, bf16[256,1536]{1,0:T(8,128)(2,1)S(1)}...) custom-call(bf16[256,1536]{1,0:T(8,128)(2,1)} %copy-done.77, ...), custom_call_target="tpu_custom_call" | custom-call | flops 15300820992 | bytes 15728640 | tf_op jit(solution)/shard_map/experts/pallas_call | solution.py:130
  183.7 1.6 collective-permute-start.14
  186.2 19.8 %experts.8 = (bf16[256,1664]{1,0:T(8,128)(2,1)}, bf16[256,1664]{1,0:T(8,128)(2,1)}, bf16[256,1536]{1,0:T(8,128)(2,1)S(1)}, bf16[256,1536]{1,0:T(8,128)(2,1)S(1)}...) custom-call(bf16[256,1536]{1,0:T(8,128)(2,1)} %copy-done.65, ...), custom_call_target="tpu_custom_call" | custom-call | flops 15300820992 | bytes 15728640 | tf_op jit(solution)/shard_map/experts/pallas_call | solution.py:130
  206.1 13.2 %experts.9 = (bf16[128,1664]{1,0:T(8,128)(2,1)}, bf16[128,1664]{1,0:T(8,128)(2,1)}, bf16[128,1536]{1,0:T(8,128)(2,1)S(1)}, bf16[128,1536]{1,0:T(8,128)(2,1)S(1)}...) custom-call(bf16[128,1536]{1,0:T(8,128)(2,1)S(1)} %collective-permute-done.14.refs_0_.refs_7_, ...), custom_call_target="tpu_custom_call" | custom-call | flops 7650410496 | bytes 12582912 | tf_op jit(solution)/shard_map/experts/pallas_call | solution.py:130
  219.3 1.6 collective-permute-start.21
  221.5 10.1 %collective-permute-done.21 = bf16[128,1664]{1,0:T(8,128)(2,1)S(1)} collective-permute-done((bf16[128,1664]{1,0:T(8,128)(2,1)}, bf16[128,1664]{1,0:T(8,128)(2,1)S(1)}, u32[]{:S(2)}, u32[]{:S(2)}) %collective-permute-start.21) | collective-permute-done | bytes 426016 | tf_op jit(solution)/shard_map/ppermute | solution.py:49
  232.7 1.8 collective-permute-start.22
  238.3 12.3 %collective-permute-done.22 = bf16[256,1664]{1,0:T(8,128)(2,1)} collective-permute-done((bf16[256,1664]{1,0:T(8,128)(2,1)}, bf16[256,1664]{1,0:T(8,128)(2,1)}, u32[]{:S(2)}, u32[]{:S(2)}) %collective-permute-start.22) | collective-permute-done | bytes 852000 | tf_op jit(solution)/shard_map/ppermute | solution.py:49
  252.0 1.9 collective-permute-start.23
  253.8 4.0 collective-permute-done.26
  259.7 11.4 %outer_products.5 = bf16[2,512,1536]{2,1,0:T(8,128)(2,1)} custom-call(bf16[256,1024]{1,0:T(8,128)(2,1)S(1)} %copy-done.41, bf16[512,1024]{1,0:T(8,128)(2,1)} %get-tuple-element.85.refs_9_.refs_1_, bf16[512,1024]{1,0:T(8,128)(2,1)} %get-tuple-element.86.refs_9_.refs_2_, bf16[512,1024]{1,0:T(8,128)(2,1)} %get-tuple-element.87.refs_9_.refs_3_, ...), custom_call_target="tpu_custom_call" | custom-call | flops 11274289152 | bytes 12000000 | tf_op jit(solution)/shard_map/outer_products/pallas_call | solution.py:130
  271.4 2.1 collective-permute-start.24
  273.5 7.8 %collective-permute-done.27 = bf16[256,1664]{1,0:T(8,128)(2,1)S(1)} collective-permute-done((bf16[256,1664]{1,0:T(8,128)(2,1)S(1)}, bf16[256,1664]{1,0:T(8,128)(2,1)S(1)}, u32[]{:S(2)}, u32[]{:S(2)}) %collective-permute-start.27) | collective-permute-done | bytes 852000 | tf_op jit(solution)/shard_map/ppermute | solution.py:49
  281.8 10.9 %outer_products.3 = bf16[2,1536,512]{2,1,0:T(8,128)(2,1)} custom-call(bf16[256,1536]{1,0:T(8,128)(2,1)} %copy-done.11, bf16[256,1536]{1,0:T(8,128)(2,1)} %collective-permute-done.11.refs_0_.refs_1_, bf16[256,1536]{1,0:T(8,128)(2,1)} %collective-permute-done.15.refs_1_.refs_2_, bf16[256,1536]{1,0:T(8,128)(2,1)} %copy-done.77, bf16[256,1536]{1,0:T(8,128)(2,1)} %copy-done.78, ...), custom_call_target="tpu_custom_call" | custom-call | flops 11274289152 | bytes 12000000 | tf_op jit(solution)/shard_map/outer_products/pallas_call | solution.py:130
  294.2 6.6 %collective-permute-done.28.refs_2_ = bf16[256,1664]{1,0:T(8,128)(2,1)S(1)} collective-permute-done((bf16[256,1664]{1,0:T(8,128)(2,1)S(1)}, bf16[256,1664]{1,0:T(8,128)(2,1)S(1)}, u32[]{:S(2)}, u32[]{:S(2)}) %collective-permute-start.28) | collective-permute-done | bytes 852000 | tf_op jit(solution)/shard_map/ppermute | solution.py:49
  301.7 6.0 %middle.1 = (f32[256,1536]{1,0:T(8,128)}, bf16[256,1536]{1,0:T(8,128)(2,1)}, f32[1,1536]{1,0:T(1,128)S(1)}, f32[16,1536]{1,0:T(8,128)S(1)}, bf16[128,1536]{1,0:T(8,128)(2,1)S(1)}) custom-call(bf16[256,1664]{1,0:T(8,128)(2,1)} %get-tuple-element.83.refs_0_, bf16[256,1664]{1,0:T(8,128)(2,1)} %copy-done.75, ...), custom_call_target="tpu_custom_call", output_to_operand_aliasing={{4}: (8, {})} | custom-call | flops 4400000000 | bytes 4000000 | tf_op jit(solution)/shard_map/middle/pallas_call | solution.py:130
  309.0 10.8 %outer_products.4 = bf16[2,1536,512]{2,1,0:T(8,128)(2,1)} custom-call(bf16[256,1536]{1,0:T(8,128)(2,1)} %copy-done.11, bf16[256,1536]{1,0:T(8,128)(2,1)} %collective-permute-done.11.refs_0_.refs_1_, bf16[256,1536]{1,0:T(8,128)(2,1)} %collective-permute-done.15.refs_1_.refs_2_, bf16[256,1536]{1,0:T(8,128)(2,1)} %copy-done.77, bf16[256,1536]{1,0:T(8,128)(2,1)} %copy-done.78, ...), custom_call_target="tpu_custom_call" | custom-call | flops 11274289152 | bytes 12000000 | tf_op jit(solution)/shard_map/outer_products/pallas_call | solution.py:130
  324.4 7.1 %collective-permute-done.29 = bf16[128,1536]{1,0:T(8,128)(2,1)S(1)} collective-permute-done((bf16[128,1536]{1,0:T(8,128)(2,1)S(1)}, bf16[128,1536]{1,0:T(8,128)(2,1)S(1)}, u32[]{:S(2)}, u32[]{:S(2)}) %collective-permute-start.29) | collective-permute-done | bytes 393248 | tf_op jit(solution)/shard_map/ppermute | solution.py:49
  331.6 1.9 collective-permute-start.30
  334.7 15.9 %attend_back.1.refs_1_.refs_11_ = bf16[1024,640]{1,0:T(8,128)(2,1)} custom-call(s32[1]{0:T(128)} %bitcast.refs_0_, bf16[256,1536]{1,0:T(8,128)(2,1)} %get-tuple-element.105.refs_1_.refs_6_, bf16[256,1536]{1,0:T(8,128)(2,1)} %copy-done.79, bf16[256,1536]{1,0:T(8,128)(2,1)} %collective-permute-done.38.refs_3_.refs_8_, bf16[256,1536]{1,0:T(8,128)(2,1)} %copy-done.80, ...), custom_call_target="tpu_custom_call" | custom-call | flops 16499999744 | bytes 12000000 | tf_op jit(solution)/shard_map/attend_back/pallas_call | solution.py:130
  350.6 10.4 %head_grads.1 = (bf16[1536,128]{1,0:T(8,128)(2,1)S(1)}, bf16[1536,128]{1,0:T(8,128)(2,1)S(1)}, bf16[1536,128]{1,0:T(8,128)(2,1)S(1)}, bf16[1536,128]{1,0:T(8,128...) custom-call(s32[1]{0:T(128)} %bitcast.refs_0_, ...), custom_call_target="tpu_custom_call" | custom-call | flops 6600000000 | bytes 12000000 | tf_op jit(solution)/shard_map/head_grads/pallas_call | solution.py:130
  366.3 3.3 collective-permute-done.51
  370.6 15.0 %collective-permute-done.47 = bf16[768,128]{1,0:T(8,128)(2,1)S(1)} collective-permute-done((bf16[768,128]{1,0:T(8,128)(2,1)S(1)}, bf16[768,128]{1,0:T(8,128)(2,1)S(1)}, u32[]{:S(2)}, u32[]{:S(2)}) %collective-permute-start.47) | collective-permute-done | bytes 196640 | tf_op jit(solution)/shard_map/ppermute | solution.py:49
  389.1 8.6 %collective-permute-done.48 = bf16[1536,128]{1,0:T(8,128)(2,1)S(1)} collective-permute-done((bf16[1536,128]{1,0:T(8,128)(2,1)S(1)}, bf16[1536,128]{1,0:T(8,128)(2,1)S(1)}, u32[]{:S(2)}, u32[]{:S(2)}) %collective-permute-start.48) | collective-permute-done | bytes 393248 | tf_op jit(solution)/shard_map/ppermute | solution.py:49
  399.1 2.5 collective-permute-start.54
  401.7 6.4 %collective-permute-done.49 = bf16[1536,128]{1,0:T(8,128)(2,1)S(1)} collective-permute-done((bf16[1536,128]{1,0:T(8,128)(2,1)S(1)}, bf16[1536,128]{1,0:T(8,128)(2,1)S(1)}, u32[]{:S(2)}, u32[]{:S(2)}) %collective-permute-start.49) | collective-permute-done | bytes 393248 | tf_op jit(solution)/shard_map/ppermute | solution.py:49
  408.3 6.4 %lin_back.1 = (bf16[2,256,1536]{2,1,0:T(8,128)(2,1)}, bf16[2,256,1536]{2,1,0:T(8,128)(2,1)}) custom-call(s32[1]{0:T(128)} %bitcast.refs_0_, bf16[1024,640]{1,0:T(8,128)(2,1)} %attend_back.1.refs_1_.refs_11_, bf16[1536,384]{1,0:T(8,128)(2,1)S(1)} %copy-done.8, bf16[1536,128]{1,0:T(8,128)(2,1)S(1)} %copy-done.17, bf16[1536,128]{1,0:T(8,128)(2,1)S(1)} %copy-done.19), custom_call_target="tpu_custom_call" | custom-call | flops 4400000000 | bytes 9000000 | tf_op jit(solution)/shard_map/lin_back/pallas_call | solution.py:130
  415.6 2.0 collective-permute-done.50
  417.8 2.0 collective-permute-start.58
  421.4 2.0 collective-permute-start.36
  423.8 6.1 %collective-permute-done.55.refs_2_ = bf16[1536,128]{1,0:T(8,128)(2,1)S(1)} collective-permute-done((bf16[1536,128]{1,0:T(8,128)(2,1)S(1)}, bf16[1536,128]{1,0:T(8,128)(2,1)S(1)}, u32[]{:S(2)}, u32[]{:S(2)}) %collective-permute-start.55) | collective-permute-done | bytes 393248 | tf_op jit(solution)/shard_map/ppermute | solution.py:49
  429.9 2.0 collective-permute-start.59
  432.1 20.7 %collective-permute-done.46 = f32[18,1536]{1,0:T(8,128)S(1)} collective-permute-done((f32[18,1536]{1,0:T(8,128)S(1)}, f32[18,1536]{1,0:T(8,128)S(1)}, u32[]{:S(2)}, u32[]{:S(2)}) %collective-permute-start.46) | collective-permute-done | bytes 110624 | tf_op jit(solution)/shard_map/ppermute | solution.py:99
  453.9 2.4 split_add.3
  456.4 1.6 collective-permute-start.41
  458.0 2.0 collective-permute-start.57
  461.3 14.1 %collective-permute-done.60.refs_7_ = bf16[1536,128]{1,0:T(8,128)(2,1)S(1)} collective-permute-done((bf16[1536,128]{1,0:T(8,128)(2,1)S(1)}, bf16[1536,128]{1,0:T(8,128)(2,1)S(1)}, u32[]{:S(2)}, u32[]{:S(2)}) %collective-permute-start.60) | collective-permute-done | bytes 393248 | tf_op jit(solution)/shard_map/ppermute | solution.py:49
  476.2 2.5 collective-permute-start.61
  480.7 29.0 %all-reduce.4.cloned.1.call-done = (bf16[2,1536,512]{2,1,0:T(8,128)(2,1)}, bf16[2,1536,512]{2,1,0:T(8,128)(2,1)}, bf16[2,512,1536]{2,1,0:T(8,128)(2,1)}) async-done(((bf16[2,1536,512]{2,1,0:T(8,128)(2,1)}, bf16[2,1536,512]{2,1,0:T(8,128)(2,1)}, bf16[2,512,1536]{2,1,0:T(8,128)(2,1)}), (bf16[2,1536,512]{2,1,0:T(8,128)(2,1)}, bf16[2,1536,512]{2,1,0:T(8,128)(2,1)}, ...) | async-done | bytes 9437200 | tf_op jit(solution)/shard_map/psum | solution.py:922
  509.7 8.4 %widen.3 = f32[2,1536,512]{2,1,0:T(8,128)} custom-call(bf16[2,1536,512]{2,1,0:T(8,128)(2,1)} %get-tuple-element.144.refs_0_, bf16[1536,128]{1,0:T(8,128)(2,1)S(1)} %collective-permute-done.58.refs_9_.refs_1_, bf16[1536,128]{1,0:T(8,128)(2,1)S(1)} %collective-permute-done.55.refs_2_), custom_call_target="tpu_custom_call" | custom-call | flops 100000000 | bytes 10000000 | tf_op jit(solution)/shard_map/widen/pallas_call | solution.py:130
  518.1 8.4 %widen.4 = f32[2,1536,512]{2,1,0:T(8,128)} custom-call(bf16[2,1536,512]{2,1,0:T(8,128)(2,1)} %get-tuple-element.145.refs_0_, bf16[1536,128]{1,0:T(8,128)(2,1)S(1)} %collective-permute-done.58.refs_9_.refs_1_, bf16[1536,128]{1,0:T(8,128)(2,1)S(1)} %collective-permute-done.55.refs_2_), custom_call_target="tpu_custom_call" | custom-call | flops 100000000 | bytes 10000000 | tf_op jit(solution)/shard_map/widen/pallas_call | solution.py:130
  526.5 5.1 widen.5
  531.7 3.3 last.1
  534.9 4.4 head_place.1
  (315 shorter events, 62.0 us)
Async XLA Ops:
  7.2 502.5 %all-reduce.4.cloned.1.call-start = ((), (), s32[]{:S(2)}) async-start(), calls=%async_computation | async-start | bytes 18874368 | tf_op jit(solution)/shard_map/psum | solution.py:922
  9.7 20.7 %collective-permute-start.1 = (bf16[256,1536]{1,0:T(8,128)(2,1)S(1)}, bf16[256,1536]{1,0:T(8,128)(2,1)}, u32[]{:S(2)}, u32[]{:S(2)}) collective-permute-start(bf16[256,1536]{1,0:T(8,128)(2,1)S(1)} %first_norm.1.refs_1_.refs_2_), channel_id=1, source_target_pairs={{0,2},{1,3},{2,0},{3,1},{4,6},{5,7},{6,4},{7,5},{8,10},{9,11},{10,... | collective-permute-start | bytes 2359304 | tf_op jit(solution)/shard_map/ppermute | solution.py:99
  13.4 20.5 %collective-permute-start.3 = (bf16[256,1664]{1,0:T(8,128)(2,1)S(1)}, bf16[256,1664]{1,0:T(8,128)(2,1)S(1)}, u32[]{:S(2)}, u32[]{:S(2)}) collective-permute-start(bf16[256,1664]{1,0:T(8,128)(2,1)S(1)} %pad_maximum_fusion.refs_1_.refs_5_), channel_id=1, source_target_pairs={{0,8},{8,16},{16,24},{24,28},{28,20},{20,12},{12,4},{4,0},{1,9},{9... | collective-permute-start | bytes 2555912 | tf_op jit(solution)/shard_map/ppermute | solution.py:49
  15.0 20.2 %collective-permute-start.4 = (bf16[256,1664]{1,0:T(8,128)(2,1)S(1)}, bf16[256,1664]{1,0:T(8,128)(2,1)}, u32[]{:S(2)}, u32[]{:S(2)}) collective-permute-start(bf16[256,1664]{1,0:T(8,128)(2,1)S(1)} %pad_maximum_fusion.refs_1_.refs_5_), channel_id=1, source_target_pairs={{0,4},{8,0},{16,8},{24,16},{28,24},{20,28},{12,20},{4,12},{1,5},{9... | collective-permute-start | bytes 2555912 | tf_op jit(solution)/shard_map/ppermute | solution.py:49
  15.4 14.9 %collective-permute-start = (bf16[256,1536]{1,0:T(8,128)(2,1)S(1)}, bf16[256,1536]{1,0:T(8,128)(2,1)}, u32[]{:S(2)}, u32[]{:S(2)}) collective-permute-start(bf16[256,1536]{1,0:T(8,128)(2,1)S(1)} %first_norm.1.refs_1_.refs_2_), channel_id=1, source_target_pairs={{0,1},{1,0},{2,3},{3,2},{4,5},{5,4},{6,7},{7,6},{8,9},{9,8},{10,11... | collective-permute-start | bytes 2359304 | tf_op jit(solution)/shard_map/ppermute | solution.py:99
  30.3 4.9 collective-permute-start.2
  56.9 26.8 %collective-permute-start.7 = (bf16[2,256,1536]{2,1,0:T(8,128)(2,1)}, bf16[2,256,1536]{2,1,0:T(8,128)(2,1)S(1)}, u32[]{:S(2)}, u32[]{:S(2)}) collective-permute-start(bf16[2,256,1536]{2,1,0:T(8,128)(2,1)} %branch.3), channel_id=1, source_target_pairs={{0,1},{1,0},{2,3},{3,2},{4,5},{5,4},{6,7},{7,6},{8,9},{9,8},{10,11... | collective-permute-start | bytes 4718600 | tf_op jit(solution)/shard_map/ppermute | solution.py:99
  56.9 21.4 %collective-permute-start.5 = (bf16[256,1664]{1,0:T(8,128)(2,1)S(1)}, bf16[256,1664]{1,0:T(8,128)(2,1)S(1)}, u32[]{:S(2)}, u32[]{:S(2)}) collective-permute-start(bf16[256,1664]{1,0:T(8,128)(2,1)S(1)} %copy-done.74), channel_id=1, source_target_pairs={{0,8},{8,16},{16,24},{24,28},{28,20},{20,12},{12,4},{4,0},{1,9},{9... | collective-permute-start | bytes 2555912 | tf_op jit(solution)/shard_map/ppermute | solution.py:49
  58.5 21.3 %collective-permute-start.6 = (bf16[256,1664]{1,0:T(8,128)(2,1)}, bf16[256,1664]{1,0:T(8,128)(2,1)}, u32[]{:S(2)}, u32[]{:S(2)}) collective-permute-start(bf16[256,1664]{1,0:T(8,128)(2,1)} %collective-permute-done.4.refs_12_.refs_3_.refs_7_), channel_id=1, source_target_pairs={{0,4},{8,0},{16,8},{24,16},{28,24},{20,28},{12,20},{4,12},{1,5},{9... | collective-permute-start | bytes 2555912 | tf_op jit(solution)/shard_map/ppermute | solution.py:49
  78.3 20.6 %collective-permute-start.9 = (bf16[256,1664]{1,0:T(8,128)(2,1)S(1)}, bf16[256,1664]{1,0:T(8,128)(2,1)S(1)}, u32[]{:S(2)}, u32[]{:S(2)}) collective-permute-start(bf16[256,1664]{1,0:T(8,128)(2,1)S(1)} %collective-permute-done.5.refs_3_.refs_2_.refs_8_), channel_id=1, source_target_pairs={{0,8},{8,16},{16,24},{24,28},{28,20},{20,12},{12,4},{4,0},{1,9},{9... | collective-permute-start | bytes 2555912 | tf_op jit(solution)/shard_map/ppermute | solution.py:49
  79.9 20.6 %collective-permute-start.10 = (bf16[256,1664]{1,0:T(8,128)(2,1)}, bf16[256,1664]{1,0:T(8,128)(2,1)}, u32[]{:S(2)}, u32[]{:S(2)}) collective-permute-start(bf16[256,1664]{1,0:T(8,128)(2,1)} %collective-permute-done.6.refs_4_.refs_3_.refs_9_), channel_id=1, source_target_pairs={{0,4},{8,0},{16,8},{24,16},{28,24},{20,28},{12,20},{4,12},{1,5},{9... | collective-permute-start | bytes 2555912 | tf_op jit(solution)/shard_map/ppermute | solution.py:49
  88.0 18.7 %collective-permute-start.8 = (bf16[256,1536]{1,0:T(8,128)(2,1)S(1)}, bf16[256,1536]{1,0:T(8,128)(2,1)}, u32[]{:S(2)}, u32[]{:S(2)}) collective-permute-start(bf16[256,1536]{1,0:T(8,128)(2,1)S(1)} %get-tuple-element.79), channel_id=1, source_target_pairs={{0,2},{1,3},{2,0},{3,1},{4,6},{5,7},{6,4},{7,5},{8,10},{9,11},{10,... | collective-permute-start | bytes 2359304 | tf_op jit(solution)/shard_map/ppermute | solution.py:99
  109.8 20.6 %collective-permute-start.11 = (bf16[256,1536]{1,0:T(8,128)(2,1)S(1)}, bf16[256,1536]{1,0:T(8,128)(2,1)}, u32[]{:S(2)}, u32[]{:S(2)}) collective-permute-start(bf16[256,1536]{1,0:T(8,128)(2,1)S(1)} %get-tuple-element.81.refs_0_.refs_4_), channel_id=1, source_target_pairs={{0,8},{8,16},{16,24},{24,28},{28,20},{20,12},{12,4},{4,0},{1,9},{9... | collective-permute-start | bytes 2359304 | tf_op jit(solution)/shard_map/ppermute | solution.py:49
  111.3 20.6 %collective-permute-start.15 = (bf16[256,1536]{1,0:T(8,128)(2,1)S(1)}, bf16[256,1536]{1,0:T(8,128)(2,1)}, u32[]{:S(2)}, u32[]{:S(2)}) collective-permute-start(bf16[256,1536]{1,0:T(8,128)(2,1)S(1)} %get-tuple-element.81.refs_0_.refs_4_), channel_id=1, source_target_pairs={{0,4},{8,0},{16,8},{24,16},{28,24},{20,28},{12,20},{4,12},{1,5},{9... | collective-permute-start | bytes 2359304 | tf_op jit(solution)/shard_map/ppermute | solution.py:49
  113.2 26.1 %collective-permute-start.19 = (bf16[128,1664]{1,0:T(8,128)(2,1)S(1)}, bf16[128,1664]{1,0:T(8,128)(2,1)S(1)}, u32[]{:S(2)}, u32[]{:S(2)}) collective-permute-start(bf16[128,1664]{1,0:T(8,128)(2,1)S(1)} %slice.86), channel_id=1, source_target_pairs={{0,8},{8,16},{16,24},{24,28},{28,20},{20,12},{12,4},{4,0},{1,9},{9... | collective-permute-start | bytes 1277960 | tf_op jit(solution)/shard_map/ppermute | solution.py:49
  115.9 25.1 %collective-permute-start.20 = (bf16[128,1664]{1,0:T(8,128)(2,1)S(1)}, bf16[128,1664]{1,0:T(8,128)(2,1)S(1)}, u32[]{:S(2)}, u32[]{:S(2)}) collective-permute-start(bf16[128,1664]{1,0:T(8,128)(2,1)S(1)} %slice.87), channel_id=1, source_target_pairs={{0,4},{8,0},{16,8},{24,16},{28,24},{20,28},{12,20},{4,12},{1,5},{9... | collective-permute-start | bytes 1277960 | tf_op jit(solution)/shard_map/ppermute | solution.py:49
  130.3 31.1 %collective-permute-start.12 = (bf16[256,1536]{1,0:T(8,128)(2,1)}, bf16[256,1536]{1,0:T(8,128)(2,1)S(1)}, u32[]{:S(2)}, u32[]{:S(2)}) collective-permute-start(bf16[256,1536]{1,0:T(8,128)(2,1)} %collective-permute-done.11.refs_0_.refs_1_), channel_id=1, source_target_pairs={{0,8},{8,16},{16,24},{24,28},{28,20},{20,12},{12,4},{4,0},{1,9},{9... | collective-permute-start | bytes 2359304 | tf_op jit(solution)/shard_map/ppermute | solution.py:49
  131.9 31.1 %collective-permute-start.16 = (bf16[256,1536]{1,0:T(8,128)(2,1)}, bf16[256,1536]{1,0:T(8,128)(2,1)S(1)}, u32[]{:S(2)}, u32[]{:S(2)}) collective-permute-start(bf16[256,1536]{1,0:T(8,128)(2,1)} %collective-permute-done.15.refs_1_.refs_2_), channel_id=1, source_target_pairs={{0,4},{8,0},{16,8},{24,16},{28,24},{20,28},{12,20},{4,12},{1,5},{9... | collective-permute-start | bytes 2359304 | tf_op jit(solution)/shard_map/ppermute | solution.py:49
  161.4 22.2 %collective-permute-start.13 = (bf16[256,1536]{1,0:T(8,128)(2,1)S(1)}, bf16[256,1536]{1,0:T(8,128)(2,1)S(1)}, u32[]{:S(2)}, u32[]{:S(2)}) collective-permute-start(bf16[256,1536]{1,0:T(8,128)(2,1)S(1)} %collective-permute-done.12.refs_0_.refs_3_), channel_id=1, source_target_pairs={{0,8},{8,16},{16,24},{24,28},{28,20},{20,12},{12,4},{4,0},{1,9},{9... | collective-permute-start | bytes 2359304 | tf_op jit(solution)/shard_map/ppermute | solution.py:49
  163.1 22.2 %collective-permute-start.17 = (bf16[256,1536]{1,0:T(8,128)(2,1)S(1)}, bf16[256,1536]{1,0:T(8,128)(2,1)S(1)}, u32[]{:S(2)}, u32[]{:S(2)}) collective-permute-start(bf16[256,1536]{1,0:T(8,128)(2,1)S(1)} %collective-permute-done.16.refs_1_.refs_4_), channel_id=1, source_target_pairs={{0,4},{8,0},{16,8},{24,16},{28,24},{20,28},{12,20},{4,12},{1,5},{9... | collective-permute-start | bytes 2359304 | tf_op jit(solution)/shard_map/ppermute | solution.py:49
  183.7 22.3 %collective-permute-start.14 = (bf16[128,1536]{1,0:T(8,128)(2,1)S(1)}, bf16[128,1536]{1,0:T(8,128)(2,1)S(1)}, u32[]{:S(2)}, u32[]{:S(2)}) collective-permute-start(bf16[128,1536]{1,0:T(8,128)(2,1)S(1)} %slice.84), channel_id=1, source_target_pairs={{0,8},{8,16},{16,24},{24,28},{28,20},{20,12},{12,4},{4,0},{1,9},{9... | collective-permute-start | bytes 1179656 | tf_op jit(solution)/shard_map/ppermute | solution.py:49
  185.3 20.7 %collective-permute-start.18 = (bf16[128,1536]{1,0:T(8,128)(2,1)S(1)}, bf16[128,1536]{1,0:T(8,128)(2,1)S(1)}, u32[]{:S(2)}, u32[]{:S(2)}) collective-permute-start(bf16[128,1536]{1,0:T(8,128)(2,1)S(1)} %slice.85), channel_id=1, source_target_pairs={{0,4},{8,0},{16,8},{24,16},{28,24},{20,28},{12,20},{4,12},{1,5},{9... | collective-permute-start | bytes 1179656 | tf_op jit(solution)/shard_map/ppermute | solution.py:49
  219.3 12.3 %collective-permute-start.21 = (bf16[128,1664]{1,0:T(8,128)(2,1)}, bf16[128,1664]{1,0:T(8,128)(2,1)S(1)}, u32[]{:S(2)}, u32[]{:S(2)}) collective-permute-start(bf16[128,1664]{1,0:T(8,128)(2,1)} %get-tuple-element.88), channel_id=1, source_target_pairs={{0,8},{8,16},{16,24},{24,28},{28,20},{20,12},{12,4},{4,0},{1,9},{9... | collective-permute-start | bytes 1277960 | tf_op jit(solution)/shard_map/ppermute | solution.py:49
  221.0 13.5 %collective-permute-start.25 = (bf16[128,1664]{1,0:T(8,128)(2,1)S(1)}, bf16[128,1664]{1,0:T(8,128)(2,1)S(1)}, u32[]{:S(2)}, u32[]{:S(2)}) collective-permute-start(bf16[128,1664]{1,0:T(8,128)(2,1)S(1)} %copy-done.81), channel_id=1, source_target_pairs={{0,4},{8,0},{16,8},{24,16},{28,24},{20,28},{12,20},{4,12},{1,5},{9... | collective-permute-start | bytes 1277960 | tf_op jit(solution)/shard_map/ppermute | solution.py:49
  232.7 17.9 %collective-permute-start.22 = (bf16[256,1664]{1,0:T(8,128)(2,1)}, bf16[256,1664]{1,0:T(8,128)(2,1)}, u32[]{:S(2)}, u32[]{:S(2)}) collective-permute-start(bf16[256,1664]{1,0:T(8,128)(2,1)} %pad_maximum_fusion.1), channel_id=1, source_target_pairs={{0,8},{8,16},{16,24},{24,28},{28,20},{20,12},{12,4},{4,0},{1,9},{9... | collective-permute-start | bytes 2555912 | tf_op jit(solution)/shard_map/ppermute | solution.py:49
  235.6 22.2 %collective-permute-start.26 = (bf16[256,1664]{1,0:T(8,128)(2,1)}, bf16[256,1664]{1,0:T(8,128)(2,1)}, u32[]{:S(2)}, u32[]{:S(2)}) collective-permute-start(bf16[256,1664]{1,0:T(8,128)(2,1)} %pad_maximum_fusion.2), channel_id=1, source_target_pairs={{0,4},{8,0},{16,8},{24,16},{28,24},{20,28},{12,20},{4,12},{1,5},{9... | collective-permute-start | bytes 2555912 | tf_op jit(solution)/shard_map/ppermute | solution.py:49
  237.9 54.8 %collective-permute-start.33 = (bf16[128,1536]{1,0:T(8,128)(2,1)S(1)}, bf16[128,1536]{1,0:T(8,128)(2,1)S(1)}, u32[]{:S(2)}, u32[]{:S(2)}) collective-permute-start(bf16[128,1536]{1,0:T(8,128)(2,1)S(1)} %copy-done.29), channel_id=1, source_target_pairs={{0,4},{8,0},{16,8},{24,16},{28,24},{20,28},{12,20},{4,12},{1,5},{9... | collective-permute-start | bytes 1179656 | tf_op jit(solution)/shard_map/ppermute | solution.py:49
  252.0 19.2 %collective-permute-start.23 = (bf16[256,1664]{1,0:T(8,128)(2,1)S(1)}, bf16[256,1664]{1,0:T(8,128)(2,1)S(1)}, u32[]{:S(2)}, u32[]{:S(2)}) collective-permute-start(bf16[256,1664]{1,0:T(8,128)(2,1)S(1)} %add_convert_fusion.3), channel_id=1, source_target_pairs={{0,8},{8,16},{16,24},{24,28},{28,20},{20,12},{12,4},{4,0},{1,9},{9... | collective-permute-start | bytes 2555912 | tf_op jit(solution)/shard_map/ppermute | solution.py:49
  259.1 22.2 %collective-permute-start.27 = (bf16[256,1664]{1,0:T(8,128)(2,1)S(1)}, bf16[256,1664]{1,0:T(8,128)(2,1)S(1)}, u32[]{:S(2)}, u32[]{:S(2)}) collective-permute-start(bf16[256,1664]{1,0:T(8,128)(2,1)S(1)} %add_convert_fusion.1), channel_id=1, source_target_pairs={{0,4},{8,0},{16,8},{24,16},{28,24},{20,28},{12,20},{4,12},{1,5},{9... | collective-permute-start | bytes 2555912 | tf_op jit(solution)/shard_map/ppermute | solution.py:49
  271.4 22.8 %collective-permute-start.24 = (bf16[256,1664]{1,0:T(8,128)(2,1)S(1)}, bf16[256,1664]{1,0:T(8,128)(2,1)S(1)}, u32[]{:S(2)}, u32[]{:S(2)}) collective-permute-start(bf16[256,1664]{1,0:T(8,128)(2,1)S(1)} %add_convert_fusion.2), channel_id=1, source_target_pairs={{0,8},{8,16},{16,24},{24,28},{28,20},{20,12},{12,4},{4,0},{1,9},{9... | collective-permute-start | bytes 2555912 | tf_op jit(solution)/shard_map/ppermute | solution.py:49
  281.5 19.2 %collective-permute-start.28 = (bf16[256,1664]{1,0:T(8,128)(2,1)S(1)}, bf16[256,1664]{1,0:T(8,128)(2,1)S(1)}, u32[]{:S(2)}, u32[]{:S(2)}) collective-permute-start(bf16[256,1664]{1,0:T(8,128)(2,1)S(1)} %add_convert_fusion), channel_id=1, source_target_pairs={{0,4},{8,0},{16,8},{24,16},{28,24},{20,28},{12,20},{4,12},{1,5},{9... | collective-permute-start | bytes 2555912 | tf_op jit(solution)/shard_map/ppermute | solution.py:49
  293.8 28.5 %collective-permute-start.34 = (bf16[256,1536]{1,0:T(8,128)(2,1)}, bf16[256,1536]{1,0:T(8,128)(2,1)}, u32[]{:S(2)}, u32[]{:S(2)}) collective-permute-start(bf16[256,1536]{1,0:T(8,128)(2,1)} %pad_maximum_fusion.4), channel_id=1, source_target_pairs={{0,4},{8,0},{16,8},{24,16},{28,24},{20,28},{12,20},{4,12},{1,5},{9... | collective-permute-start | bytes 2359304 | tf_op jit(solution)/shard_map/ppermute | solution.py:49
  308.5 13.8 %collective-permute-start.38 = (bf16[256,1536]{1,0:T(8,128)(2,1)}, bf16[256,1536]{1,0:T(8,128)(2,1)}, u32[]{:S(2)}, u32[]{:S(2)}) collective-permute-start(bf16[256,1536]{1,0:T(8,128)(2,1)} %get-tuple-element.105.refs_1_.refs_6_), channel_id=1, source_target_pairs={{0,2},{1,3},{2,0},{3,1},{4,6},{5,7},{6,4},{7,5},{8,10},{9,11},{10,... | collective-permute-start | bytes 2359304 | tf_op jit(solution)/shard_map/ppermute | solution.py:99
  319.9 13.6 %collective-permute-start.37 = (bf16[256,1536]{1,0:T(8,128)(2,1)}, bf16[256,1536]{1,0:T(8,128)(2,1)S(1)}, u32[]{:S(2)}, u32[]{:S(2)}) collective-permute-start(bf16[256,1536]{1,0:T(8,128)(2,1)} %get-tuple-element.105.refs_1_.refs_6_), channel_id=1, source_target_pairs={{0,1},{1,0},{2,3},{3,2},{4,5},{5,4},{6,7},{7,6},{8,9},{9,8},{10,11... | collective-permute-start | bytes 2359304 | tf_op jit(solution)/shard_map/ppermute | solution.py:99
  320.8 10.6 %collective-permute-start.29 = (bf16[128,1536]{1,0:T(8,128)(2,1)S(1)}, bf16[128,1536]{1,0:T(8,128)(2,1)S(1)}, u32[]{:S(2)}, u32[]{:S(2)}) collective-permute-start(bf16[128,1536]{1,0:T(8,128)(2,1)S(1)} %copy-done.27), channel_id=1, source_target_pairs={{0,8},{8,16},{16,24},{24,28},{28,20},{20,12},{12,4},{4,0},{1,9},{9... | collective-permute-start | bytes 1179656 | tf_op jit(solution)/shard_map/ppermute | solution.py:49
  322.3 11.3 %collective-permute-start.39 = (bf16[256,1536]{1,0:T(8,128)(2,1)}, bf16[256,1536]{1,0:T(8,128)(2,1)S(1)}, u32[]{:S(2)}, u32[]{:S(2)}) collective-permute-start(bf16[256,1536]{1,0:T(8,128)(2,1)} %collective-permute-done.38.refs_3_.refs_8_), channel_id=1, source_target_pairs={{0,1},{1,0},{2,3},{3,2},{4,5},{5,4},{6,7},{7,6},{8,9},{9,8},{10,11... | collective-permute-start | bytes 2359304 | tf_op jit(solution)/shard_map/ppermute | solution.py:99
  323.7 94.1 %collective-permute-start.35 = (bf16[256,1536]{1,0:T(8,128)(2,1)S(1)}, bf16[256,1536]{1,0:T(8,128)(2,1)S(1)}, u32[]{:S(2)}, u32[]{:S(2)}) collective-permute-start(bf16[256,1536]{1,0:T(8,128)(2,1)S(1)} %add_convert_fusion.6), channel_id=1, source_target_pairs={{0,4},{8,0},{16,8},{24,16},{28,24},{20,28},{12,20},{4,12},{1,5},{9... | collective-permute-start | bytes 2359304 | tf_op jit(solution)/shard_map/ppermute | solution.py:49
  331.6 29.5 %collective-permute-start.30 = (bf16[256,1536]{1,0:T(8,128)(2,1)S(1)}, bf16[256,1536]{1,0:T(8,128)(2,1)S(1)}, u32[]{:S(2)}, u32[]{:S(2)}) collective-permute-start(bf16[256,1536]{1,0:T(8,128)(2,1)S(1)} %pad_maximum_fusion.3), channel_id=1, source_target_pairs={{0,8},{8,16},{16,24},{24,28},{28,20},{20,12},{12,4},{4,0},{1,9},{9... | collective-permute-start | bytes 2359304 | tf_op jit(solution)/shard_map/ppermute | solution.py:49
  361.0 3.6 collective-permute-start.42
  361.3 62.1 %collective-permute-start.31 = (bf16[256,1536]{1,0:T(8,128)(2,1)S(1)}, bf16[256,1536]{1,0:T(8,128)(2,1)S(1)}, u32[]{:S(2)}, u32[]{:S(2)}) collective-permute-start(bf16[256,1536]{1,0:T(8,128)(2,1)S(1)} %add_convert_fusion.8), channel_id=1, source_target_pairs={{0,8},{8,16},{16,24},{24,28},{28,20},{20,12},{12,4},{4,0},{1,9},{9... | collective-permute-start | bytes 2359304 | tf_op jit(solution)/shard_map/ppermute | solution.py:49
  362.5 7.0 %collective-permute-start.51 = (bf16[768,128]{1,0:T(8,128)(2,1)S(1)}, bf16[768,128]{1,0:T(8,128)(2,1)S(1)}, u32[]{:S(2)}, u32[]{:S(2)}) collective-permute-start(bf16[768,128]{1,0:T(8,128)(2,1)S(1)} %get-tuple-element.124), channel_id=1, source_target_pairs={{0,4},{8,0},{16,8},{24,16},{28,24},{20,28},{12,20},{4,12},{1,5},{9... | collective-permute-start | bytes 589832 | tf_op jit(solution)/shard_map/ppermute | solution.py:49
  363.4 22.1 %collective-permute-start.47 = (bf16[768,128]{1,0:T(8,128)(2,1)S(1)}, bf16[768,128]{1,0:T(8,128)(2,1)S(1)}, u32[]{:S(2)}, u32[]{:S(2)}) collective-permute-start(bf16[768,128]{1,0:T(8,128)(2,1)S(1)} %get-tuple-element.119), channel_id=1, source_target_pairs={{0,8},{8,16},{16,24},{24,28},{28,20},{20,12},{12,4},{4,0},{1,9},{9... | collective-permute-start | bytes 589832 | tf_op jit(solution)/shard_map/ppermute | solution.py:49
  364.7 22.1 %collective-permute-start.43 = (f32[18,1536]{1,0:T(8,128)S(1)}, f32[18,1536]{1,0:T(8,128)S(1)}, u32[]{:S(2)}, u32[]{:S(2)}) collective-permute-start(f32[18,1536]{1,0:T(8,128)S(1)} %fusion.2), channel_id=1, source_target_pairs={{0,2},{1,3},{2,0},{3,1},{4,6},{5,7},{6,4},{7,5},{8,10},{9,11},{10,... | collective-permute-start | bytes 331784 | tf_op jit(solution)/shard_map/ppermute | solution.py:99
  369.6 18.2 %collective-permute-start.52 = (bf16[1536,128]{1,0:T(8,128)(2,1)S(1)}, bf16[1536,128]{1,0:T(8,128)(2,1)S(1)}, u32[]{:S(2)}, u32[]{:S(2)}) collective-permute-start(bf16[1536,128]{1,0:T(8,128)(2,1)S(1)} %pad_maximum_fusion.6), channel_id=1, source_target_pairs={{0,4},{8,0},{16,8},{24,16},{28,24},{20,28},{12,20},{4,12},{1,5},{9... | collective-permute-start | bytes 1179656 | tf_op jit(solution)/shard_map/ppermute | solution.py:49
  385.6 12.1 %collective-permute-start.48 = (bf16[1536,128]{1,0:T(8,128)(2,1)S(1)}, bf16[1536,128]{1,0:T(8,128)(2,1)S(1)}, u32[]{:S(2)}, u32[]{:S(2)}) collective-permute-start(bf16[1536,128]{1,0:T(8,128)(2,1)S(1)} %pad_maximum_fusion.5), channel_id=1, source_target_pairs={{0,8},{8,16},{16,24},{24,28},{28,20},{20,12},{12,4},{4,0},{1,9},{9... | collective-permute-start | bytes 1179656 | tf_op jit(solution)/shard_map/ppermute | solution.py:49
  386.9 27.8 %collective-permute-start.44 = (f32[18,1536]{1,0:T(8,128)S(1)}, f32[18,1536]{1,0:T(8,128)S(1)}, u32[]{:S(2)}, u32[]{:S(2)}) collective-permute-start(f32[18,1536]{1,0:T(8,128)S(1)} %add.139), channel_id=1, source_target_pairs={{0,4},{4,0},{8,12},{12,8},{16,20},{20,16},{24,28},{28,24},{1,5},{5... | collective-permute-start | bytes 331784 | tf_op jit(solution)/shard_map/ppermute | solution.py:99
  387.9 11.1 %collective-permute-start.53 = (bf16[1536,128]{1,0:T(8,128)(2,1)S(1)}, bf16[1536,128]{1,0:T(8,128)(2,1)S(1)}, u32[]{:S(2)}, u32[]{:S(2)}) collective-permute-start(bf16[1536,128]{1,0:T(8,128)(2,1)S(1)} %add_convert_fusion.13), channel_id=1, source_target_pairs={{0,4},{8,0},{16,8},{24,16},{28,24},{20,28},{12,20},{4,12},{1,5},{9... | collective-permute-start | bytes 1179656 | tf_op jit(solution)/shard_map/ppermute | solution.py:49
  397.8 10.3 %collective-permute-start.49 = (bf16[1536,128]{1,0:T(8,128)(2,1)S(1)}, bf16[1536,128]{1,0:T(8,128)(2,1)S(1)}, u32[]{:S(2)}, u32[]{:S(2)}) collective-permute-start(bf16[1536,128]{1,0:T(8,128)(2,1)S(1)} %add_convert_fusion.15), channel_id=1, source_target_pairs={{0,8},{8,16},{16,24},{24,28},{28,20},{20,12},{12,4},{4,0},{1,9},{9... | collective-permute-start | bytes 1179656 | tf_op jit(solution)/shard_map/ppermute | solution.py:49
  399.1 15.6 %collective-permute-start.54 = (bf16[1536,128]{1,0:T(8,128)(2,1)S(1)}, bf16[1536,128]{1,0:T(8,128)(2,1)S(1)}, u32[]{:S(2)}, u32[]{:S(2)}) collective-permute-start(bf16[1536,128]{1,0:T(8,128)(2,1)S(1)} %add_convert_fusion.12), channel_id=1, source_target_pairs={{0,4},{8,0},{16,8},{24,16},{28,24},{20,28},{12,20},{4,12},{1,5},{9... | collective-permute-start | bytes 1179656 | tf_op jit(solution)/shard_map/ppermute | solution.py:49
  408.2 9.4 %collective-permute-start.50 = (bf16[1536,128]{1,0:T(8,128)(2,1)S(1)}, bf16[1536,128]{1,0:T(8,128)(2,1)S(1)}, u32[]{:S(2)}, u32[]{:S(2)}) collective-permute-start(bf16[1536,128]{1,0:T(8,128)(2,1)S(1)} %add_convert_fusion.14), channel_id=1, source_target_pairs={{0,8},{8,16},{16,24},{24,28},{28,20},{20,12},{12,4},{4,0},{1,9},{9... | collective-permute-start | bytes 1179656 | tf_op jit(solution)/shard_map/ppermute | solution.py:49
  414.7 38.1 %collective-permute-start.40 = (bf16[2,256,1536]{2,1,0:T(8,128)(2,1)}, bf16[2,256,1536]{2,1,0:T(8,128)(2,1)S(1)}, u32[]{:S(2)}, u32[]{:S(2)}) collective-permute-start(bf16[2,256,1536]{2,1,0:T(8,128)(2,1)} %get-tuple-element.111), channel_id=1, source_target_pairs={{0,1},{1,0},{2,3},{3,2},{4,5},{5,4},{6,7},{7,6},{8,9},{9,8},{10,11... | collective-permute-start | bytes 4718600 | tf_op jit(solution)/shard_map/ppermute | solution.py:99
  414.7 6.7 %collective-permute-start.45 = (f32[18,1536]{1,0:T(8,128)S(1)}, f32[18,1536]{1,0:T(8,128)S(1)}, u32[]{:S(2)}, u32[]{:S(2)}) collective-permute-start(f32[18,1536]{1,0:T(8,128)S(1)} %add.140), channel_id=1, source_target_pairs={{0,8},{4,12},{8,0},{12,4},{16,24},{20,28},{24,16},{28,20},{1,9},{5... | collective-permute-start | bytes 331784 | tf_op jit(solution)/shard_map/ppermute | solution.py:99
  417.8 12.1 %collective-permute-start.55 = (bf16[1536,128]{1,0:T(8,128)(2,1)S(1)}, bf16[1536,128]{1,0:T(8,128)(2,1)S(1)}, u32[]{:S(2)}, u32[]{:S(2)}) collective-permute-start(bf16[1536,128]{1,0:T(8,128)(2,1)S(1)} %add_convert_fusion.11.refs_1_), channel_id=1, source_target_pairs={{0,4},{8,0},{16,8},{24,16},{28,24},{20,28},{12,20},{4,12},{1,5},{9... | collective-permute-start | bytes 1179656 | tf_op jit(solution)/shard_map/ppermute | solution.py:49
  417.8 12.0 %collective-permute-start.58 = (bf16[1536,128]{1,0:T(8,128)(2,1)S(1)}, bf16[1536,128]{1,0:T(8,128)(2,1)S(1)}, u32[]{:S(2)}, u32[]{:S(2)}) collective-permute-start(bf16[1536,128]{1,0:T(8,128)(2,1)S(1)} %add_convert_fusion.11.refs_1_), channel_id=1, source_target_pairs={{0,8},{8,16},{16,24},{24,28},{28,20},{20,12},{12,4},{4,0},{1,9},{9... | collective-permute-start | bytes 1179656 | tf_op jit(solution)/shard_map/ppermute | solution.py:49
  421.4 58.0 %collective-permute-start.36 = (bf16[256,1536]{1,0:T(8,128)(2,1)S(1)}, bf16[256,1536]{1,0:T(8,128)(2,1)S(1)}, u32[]{:S(2)}, u32[]{:S(2)}) collective-permute-start(bf16[256,1536]{1,0:T(8,128)(2,1)S(1)} %add_convert_fusion.5), channel_id=1, source_target_pairs={{0,4},{8,0},{16,8},{24,16},{28,24},{20,28},{12,20},{4,12},{1,5},{9... | collective-permute-start | bytes 2359304 | tf_op jit(solution)/shard_map/ppermute | solution.py:49
  423.4 29.3 %collective-permute-start.46 = (f32[18,1536]{1,0:T(8,128)S(1)}, f32[18,1536]{1,0:T(8,128)S(1)}, u32[]{:S(2)}, u32[]{:S(2)}) collective-permute-start(f32[18,1536]{1,0:T(8,128)S(1)} %add.141), channel_id=1, source_target_pairs={{0,16},{4,20},{8,24},{12,28},{16,0},{20,4},{24,8},{28,12},{1,17},{... | collective-permute-start | bytes 331784 | tf_op jit(solution)/shard_map/ppermute | solution.py:99
  429.9 28.1 %collective-permute-start.56 = (bf16[1536,128]{1,0:T(8,128)(2,1)S(1)}, bf16[1536,128]{1,0:T(8,128)(2,1)S(1)}, u32[]{:S(2)}, u32[]{:S(2)}) collective-permute-start(bf16[1536,128]{1,0:T(8,128)(2,1)S(1)} %collective-permute-done.55.refs_2_), channel_id=1, source_target_pairs={{0,4},{8,0},{16,8},{24,16},{28,24},{20,28},{12,20},{4,12},{1,5},{9... | collective-permute-start | bytes 1179656 | tf_op jit(solution)/shard_map/ppermute | solution.py:49
  429.9 30.1 %collective-permute-start.59 = (bf16[1536,128]{1,0:T(8,128)(2,1)S(1)}, bf16[1536,128]{1,0:T(8,128)(2,1)S(1)}, u32[]{:S(2)}, u32[]{:S(2)}) collective-permute-start(bf16[1536,128]{1,0:T(8,128)(2,1)S(1)} %collective-permute-done.58.refs_9_.refs_1_), channel_id=1, source_target_pairs={{0,8},{8,16},{16,24},{24,28},{28,20},{20,12},{12,4},{4,0},{1,9},{9... | collective-permute-start | bytes 1179656 | tf_op jit(solution)/shard_map/ppermute | solution.py:49
  452.8 26.6 %collective-permute-start.32 = (bf16[256,1536]{1,0:T(8,128)(2,1)S(1)}, bf16[256,1536]{1,0:T(8,128)(2,1)S(1)}, u32[]{:S(2)}, u32[]{:S(2)}) collective-permute-start(bf16[256,1536]{1,0:T(8,128)(2,1)S(1)} %add_convert_fusion.7), channel_id=1, source_target_pairs={{0,8},{8,16},{16,24},{24,28},{28,20},{20,12},{12,4},{4,0},{1,9},{9... | collective-permute-start | bytes 2359304 | tf_op jit(solution)/shard_map/ppermute | solution.py:49
  456.4 75.3 %collective-permute-start.41 = (bf16[256,1536]{1,0:T(8,128)(2,1)S(1)}, bf16[256,1536]{1,0:T(8,128)(2,1)}, u32[]{:S(2)}, u32[]{:S(2)}) collective-permute-start(bf16[256,1536]{1,0:T(8,128)(2,1)S(1)} %get-tuple-element.113), channel_id=1, source_target_pairs={{0,2},{1,3},{2,0},{3,1},{4,6},{5,7},{6,4},{7,5},{8,10},{9,11},{10,... | collective-permute-start | bytes 2359304 | tf_op jit(solution)/shard_map/ppermute | solution.py:99
  458.0 20.7 %collective-permute-start.57 = (bf16[1536,128]{1,0:T(8,128)(2,1)S(1)}, bf16[1536,128]{1,0:T(8,128)(2,1)S(1)}, u32[]{:S(2)}, u32[]{:S(2)}) collective-permute-start(bf16[1536,128]{1,0:T(8,128)(2,1)S(1)} %collective-permute-done.56.refs_3_), channel_id=1, source_target_pairs={{0,4},{8,0},{16,8},{24,16},{28,24},{20,28},{12,20},{4,12},{1,5},{9... | collective-permute-start | bytes 1179656 | tf_op jit(solution)/shard_map/ppermute | solution.py:49
  460.0 15.5 %collective-permute-start.60 = (bf16[1536,128]{1,0:T(8,128)(2,1)S(1)}, bf16[1536,128]{1,0:T(8,128)(2,1)S(1)}, u32[]{:S(2)}, u32[]{:S(2)}) collective-permute-start(bf16[1536,128]{1,0:T(8,128)(2,1)S(1)} %collective-permute-done.59.refs_8_), channel_id=1, source_target_pairs={{0,8},{8,16},{16,24},{24,28},{28,20},{20,12},{12,4},{4,0},{1,9},{9... | collective-permute-start | bytes 1179656 | tf_op jit(solution)/shard_map/ppermute | solution.py:49
  476.2 58.7 %collective-permute-start.61 = (bf16[768,128]{1,0:T(8,128)(2,1)}, bf16[768,128]{1,0:T(8,128)(2,1)}, u32[]{:S(2)}, u32[]{:S(2)}) collective-permute-start(bf16[768,128]{1,0:T(8,128)(2,1)} %slice.89), channel_id=1, source_target_pairs={{0,8},{8,16},{16,24},{24,28},{28,20},{20,12},{12,4},{4,0},{1,9},{9... | collective-permute-start | bytes 589832 | tf_op jit(solution)/shard_map/ppermute | solution.py:49
  479.4 55.6 %collective-permute-start.62 = (bf16[768,128]{1,0:T(8,128)(2,1)}, bf16[768,128]{1,0:T(8,128)(2,1)}, u32[]{:S(2)}, u32[]{:S(2)}) collective-permute-start(bf16[768,128]{1,0:T(8,128)(2,1)} %slice.90), channel_id=1, source_target_pairs={{0,4},{8,0},{16,8},{24,16},{28,24},{20,28},{12,20},{4,12},{1,5},{9... | collective-permute-start | bytes 589832 | tf_op jit(solution)/shard_map/ppermute | solution.py:49
  (84 other events, 970.6 us)
Sparse Core Ops, SparseCore 0:
  320.0 189.6 all-reduce.3
